TPU v7x, 32 devices: a whole 2x2x4 slice. The times are simulated.
32 devices in a mesh: tgt: 4 (over y, core), src: 8 (over z, x).
Axes of the slice: x: 2, y: 2, z: 4, core: 2. Of those that a mesh axis runs over, the one named last changes fastest.
Arguments:
- trial_vectors: float32 [8, 32, 128], P(None, ('tgt', 'src')), may hold values from -18 to 18
- couplings: float32 [32, 8, 128, 128], P('tgt', 'src'), may hold values from -0.25 to 0.25
- neighbours: int32 [32, 8], P('tgt', 'src'), may hold values from 0 to 31, as said below
- live_slots: int32 [32, 8], P('tgt', 'src'), may hold values from 0 to 1, as said below
- energies: float32 [32, 128], P(('tgt', 'src')), may hold values from 1 to 3
Outputs:
- sigma_vectors: float32 [8, 32, 128], P(None, ('tgt', 'src'))
- residual: float32 [8, 32, 128], P(None, ('tgt', 'src'))
- residual_norms: float32 [8], replicated
Inputs may be any that keep to these rules, and one draw needn't show every extreme that they name: `neighbours`: each entry differs from its own chromophore's index by at most 4. `live_slots`: some chromophore has all 8 slots live.
All inputs are finite; a program needn't handle non-finite values.
Results may differ from a plain program's by a relative error of at most 0.000062.
Values sent between devices are 32-bit elements; how exact they have to be, the bound alone decides.
No kernel may reach another device: no remote copies, remote signals or barrier semaphores. Data moves between devices by JAX's collectives and lax.ppermute only.
A program may use at most 64 MiB of HBM per device.

v0:
```python
import jax
import jax.numpy as jnp
from jax import lax
from jax.sharding import PartitionSpec as P


def with_halo(block, sides, width):
    for axis, dim in sides:
        count = lax.axis_size(axis)
        forward = [(i, i + 1) for i in range(count - 1)]
        backward = [(target, source) for source, target in forward]
        low = lax.ppermute(
            lax.slice_in_dim(block, block.shape[dim] - width, None, axis=dim), axis, forward
        )
        high = lax.ppermute(lax.slice_in_dim(block, 0, width, axis=dim), axis, backward)
        block = jnp.concatenate([low, block, high], axis=dim)
    return block


def shards(trial_vectors, couplings, neighbours, live_slots, energies):
    vectors = trial_vectors.shape[0]
    states = trial_vectors.shape[2]
    source_block = lax.all_gather(trial_vectors, "src", axis=1, tiled=True)
    block_len = source_block.shape[1]
    widened = with_halo(source_block, (("tgt", 1),), block_len)
    anchor = lax.axis_index("tgt") * block_len - block_len
    local_rows = neighbours - anchor
    slot_count = neighbours.shape[1]
    fetched = jnp.take(widened, local_rows.reshape(-1), axis=1)
    fetched = fetched.reshape(vectors, block_len, slot_count, states)
    fetched = fetched * live_slots.astype(jnp.float32)[None, :, :, None]
    partial_value = jnp.einsum(
        "inab,kinb->kia", couplings, fetched, precision=lax.Precision.HIGHEST
    )
    sigmas = (
        lax.psum_scatter(partial_value, "src", scatter_dimension=1, tiled=True)
        + energies[None] * trial_vectors
    )
    projected = jnp.einsum("kia,lia->kl", trial_vectors, sigmas, precision=lax.Precision.HIGHEST)
    metric = jnp.einsum(
        "kia,lia->kl", trial_vectors, trial_vectors, precision=lax.Precision.HIGHEST
    )
    squares = jnp.sum(sigmas * sigmas, axis=(1, 2))
    projected, metric, squares = lax.psum((projected, metric, squares), ("tgt", "src"))
    factor = jnp.linalg.cholesky(metric)
    mixing = jax.scipy.linalg.cho_solve((factor, True), projected)
    residual = sigmas - jnp.einsum(
        "kia,kl->lia", trial_vectors, mixing, precision=lax.Precision.HIGHEST
    )
    totals = squares - jnp.sum(projected * mixing, axis=0)
    residual_norms = jnp.sqrt(totals / jnp.diagonal(metric))
    return (sigmas, residual, residual_norms)


def solution(mesh):
    return jax.shard_map(
        shards,
        mesh=mesh,
        in_specs=(
            P(None, ("tgt", "src"), None),
            P("tgt", "src", None, None),
            P("tgt", "src"),
            P("tgt", "src"),
            P(("tgt", "src"), None),
        ),
        out_specs=(P(None, ("tgt", "src"), None), P(None, ("tgt", "src"), None), P()),
        check_vma=False,
    )
```

profile of v0, /device:TPU:0, one launch (start us, length us, event | category | flops | bytes accessed | tf_op | source)
XLA Modules:
  0.0 123.4 jit_solution(12828127240238553243)
XLA Ops:
  0.6 0.0 copy-start
  0.6 32.5 %all_gather.3 = f32[8,8,128]{2,0,1:T(8,128)S(1)} all-gather(f32[8,1,128]{2,0,1:T(8,128)} %bitcast.51), channel_id=1, replica_groups=mesh['tgt'=4,'src'=8] {'src'}, dimensions={1}, use_global_device_ids=true | all-gather | bytes 36864 | tf_op jit(solution)/shard_map/all_gather | solution.py:23
  33.1 1.3 %collective-permute-start = (f32[8,8,128]{2,0,1:T(8,128)S(1)}, f32[8,8,128]{2,0,1:T(8,128)S(1)}, u32[]{:S(2)}, u32[]{:S(2)}) collective-permute-start(f32[8,8,128]{2,0,1:T(8,128)S(1)} %all_gather.3), channel_id=1, source_target_pairs={{0,8},{8,16},{16,24},{1,9},{9,17},{17,25},{2,10},{10,18},{18,26},{... | collective-permute-start | bytes 98312 | tf_op jit(solution)/shard_map/ppermute | solution.py:12
  34.4 1.3 %collective-permute-start.1 = (f32[8,8,128]{2,0,1:T(8,128)S(1)}, f32[8,8,128]{2,0,1:T(8,128)S(1)}, u32[]{:S(2)}, u32[]{:S(2)}) collective-permute-start(f32[8,8,128]{2,0,1:T(8,128)S(1)} %all_gather.3), channel_id=1, source_target_pairs={{8,0},{16,8},{24,16},{9,1},{17,9},{25,17},{10,2},{18,10},{26,18},{... | collective-permute-start | bytes 98312 | tf_op jit(solution)/shard_map/ppermute | solution.py:15
  35.7 0.0 copy-start.4
  35.7 0.6 copy-done.4
  36.4 0.0 copy-start.5
  36.4 0.0 copy-start.1
  36.4 0.6 copy-done.5
  37.0 0.0 copy-done.1
  37.1 0.1 fusion.17
  37.2 0.0 copy-start.6
  37.2 0.6 copy-done.6
  37.9 0.6 dynamic-slice
  38.5 0.0 collective-permute-done
  38.5 0.8 collective-permute-done.1
  39.3 0.6 gather_fusion
  39.8 0.0 copy-done
  39.8 1.0 convolution_bitcast_fusion
  40.8 37.0 %all-reduce = f32[8,8,128]{2,0,1:T(8,128)S(1)} all-reduce(f32[8,8,128]{2,0,1:T(8,128)S(1)} %convolution_bitcast_fusion), channel_id=2, replica_groups=mesh['tgt'=4,'src'=8] {'src'}, use_global_device_ids=true, to_apply=%region_0.1.clone | all-reduce | flops 8192 | bytes 65536
  77.8 0.0 copy-start.3
  77.8 0.7 copy-done.3
  78.5 0.8 multiply_reduce_fusion.1
  79.3 0.0 copy-start.2
  79.3 0.1 convolution_bitcast_fusion.2
  79.4 38.7 %all-reduce.1 = (f32[8,8]{0,1:T(8,128)S(1)}, f32[8,8]{0,1:T(8,128)S(1)}, f32[8]{0:T(128)S(1)}) all-reduce(f32[8,8]{0,1:T(8,128)S(1)} %convolution_bitcast_fusion.2, f32[8,8]{0,1:T(8,128)S(1)} %fusion.17, f32[8]{0:T(128)S(1)} %get-tuple-element.15), channel_id=1, replica_groups=mesh['tgt'=4,'src'=8] {'tgt','src'}, use_global_device_ids=true, to_apply=%region_4.5 | all-reduce | flops 136 | bytes 1088 | tf_op jit(solution)/shard_map/psum | solution.py:44
  118.1 0.1 copy.27
  118.2 0.7 cholesky.16
  118.9 0.6 compare_reduce_fusion
  119.6 0.6 fusion.8
  120.2 0.6 custom-call.10
  120.9 0.2 fusion.9
  121.1 0.1 fusion.11
  121.2 0.1 copy.29
  121.3 0.0 copy-done.2
  121.3 0.8 fusion
  122.1 0.1 multiply_reduce_fusion
  122.2 0.6 gather_fusion.1
  122.8 0.5 fusion.15
  (7 shorter events, 0.1 us)
Async XLA Ops:
  0.6 39.2 %copy-start = (f32[8,1,128,128]{3,2,1,0:T(8,128)S(1)}, f32[8,1,128,128]{3,2,1,0:T(8,128)}, u32[]{:S(2)}) copy-start(f32[8,1,128,128]{3,2,1,0:T(8,128)} %param.6) | copy-start | bytes 1572868
  33.1 5.4 %collective-permute-start = (f32[8,8,128]{2,0,1:T(8,128)S(1)}, f32[8,8,128]{2,0,1:T(8,128)S(1)}, u32[]{:S(2)}, u32[]{:S(2)}) collective-permute-start(f32[8,8,128]{2,0,1:T(8,128)S(1)} %all_gather.3), channel_id=1, source_target_pairs={{0,8},{8,16},{16,24},{1,9},{9,17},{17,25},{2,10},{10,18},{18,26},{... | collective-permute-start | bytes 98312 | tf_op jit(solution)/shard_map/ppermute | solution.py:12
  34.4 4.9 %collective-permute-start.1 = (f32[8,8,128]{2,0,1:T(8,128)S(1)}, f32[8,8,128]{2,0,1:T(8,128)S(1)}, u32[]{:S(2)}, u32[]{:S(2)}) collective-permute-start(f32[8,8,128]{2,0,1:T(8,128)S(1)} %all_gather.3), channel_id=1, source_target_pairs={{8,0},{16,8},{24,16},{9,1},{17,9},{25,17},{10,2},{18,10},{26,18},{... | collective-permute-start | bytes 98312 | tf_op jit(solution)/shard_map/ppermute | solution.py:15
  35.7 0.7 copy-start.4
  36.4 0.7 copy-start.5
  36.4 0.7 copy-start.1
  37.2 0.7 copy-start.6
  77.8 0.7 copy-start.3
  79.3 42.0 %copy-start.2 = (f32[8,1,128]{2,0,1:T(8,128)}, f32[8,1,128]{2,0,1:T(8,128)S(1)}, u32[]{:S(2)}) copy-start(f32[8,1,128]{2,0,1:T(8,128)S(1)} %get-tuple-element.16) | copy-start | bytes 12292
where the time goes:
time: 125 us; the launch traced here: 123 us
  blocking collectives  108 us (86%)
  local copies, waits for them, and re-layouts  4.56 us (4%)
  other arithmetic  4.12 us (3%)
  starting transfers between devices  2.57 us (2%)
  matrix products  2.34 us (2%)
    psum x1, blocking collectives, shards(): lax.psum((projected, metric, squares), ('tgt', 'src'))  38.7 us
    unnamed x1, blocking collectives  37 us
    all_gather x1, blocking collectives, shards(): source_block = lax.all_gather(trial_vectors, 'src', axis=1, tiled=True)  32.5 us
    unnamed x15, local copies, waits for them, and re-layouts  3.23 us
  transfers between devices with their start and end apart: 2, of which 1 were waited for; matrix products, arithmetic and copies ran while one was open for 1% of the time, Pallas kernels for 0%

commit v1 on v0

v1 whole, which is shorter than its diff:
```python
import functools

import jax
import jax.numpy as jnp
from jax import lax
from jax.experimental import pallas as pl
from jax.experimental.pallas import tpu as pltpu
from jax.sharding import PartitionSpec as P

HIGHEST = lax.Precision.HIGHEST
VMEM = pl.BlockSpec(memory_space=pltpu.VMEM)
SMEM = pl.BlockSpec(memory_space=pltpu.SMEM)
LIMIT = 24 * 2**20


def exchange(x, axis, bit):
    count = lax.axis_size(axis)
    return lax.ppermute(x, axis, [(i, i ^ bit) for i in range(count)])


def bits_of(count):
    return [1 << n for n in range(count.bit_length() - 1)]


def place_of(relative, order):
    place = 0
    for n, bit in enumerate(order):
        place = place + jnp.where((relative & bit) != 0, 1 << n, 0)
    return place


def products(order, table, couplings, neighbours, live, energies, partial, block):
    targets, slots = couplings.shape[0], couplings.shape[1]
    own_src = lax.axis_index("src")
    first = lax.axis_index("tgt") * targets
    own = first + own_src
    for i in range(targets):
        block[i] = table[place_of(own ^ (first + i), order)]
        total = None
        for n in range(slots):
            row = table[place_of(own ^ neighbours[i, n], order)]
            row = row * live[i, n].astype(jnp.float32)
            term = lax.dot_general(
                row,
                couplings[i, n],
                (((1,), (1,)), ((), ())),
                precision=HIGHEST,
                preferred_element_type=jnp.float32,
            )
            total = term if total is None else total + term
        partial[i] = total
    partial[own_src] = partial[own_src] + table[0] * energies[...]


def lanes_of(ref):
    return jnp.concatenate([ref[i] for i in range(ref.shape[0])], axis=1)


def contract(left, right):
    return lax.dot_general(
        left,
        right,
        (((1,), (1,)), ((), ())),
        precision=HIGHEST,
        preferred_element_type=jnp.float32,
    )


def invert(table, out):
    rows, vectors, states = table.shape
    metric = jnp.zeros((vectors, vectors), jnp.float32)
    step = 32
    for r in range(0, rows, step):
        part = jnp.concatenate([table[i] for i in range(r, min(r + step, rows))], axis=1)
        metric = metric + contract(part, part)
    eye = (
        lax.broadcasted_iota(jnp.int32, (vectors, vectors), 0)
        == lax.broadcasted_iota(jnp.int32, (vectors, vectors), 1)
    )
    diagonal = jnp.sum(jnp.where(eye, metric, 0.0), axis=1, keepdims=True)
    sublane = lax.broadcasted_iota(jnp.int32, (vectors, states), 0)
    right = table[0]
    lane = lax.broadcasted_iota(jnp.int32, (vectors, states), 1)
    wide = jnp.concatenate(
        [metric, jnp.where(eye, 1.0, 0.0), jnp.zeros((vectors, states - 2 * vectors), jnp.float32)],
        axis=1,
    )
    for j in range(vectors):
        column = wide[:, j : j + 1]
        inverse = 1.0 / wide[j : j + 1, j : j + 1]
        pivot = wide[j : j + 1, :] * inverse
        pivot_right = right[j : j + 1, :] * inverse
        wide = jnp.where(sublane == j, pivot, wide - column * pivot)
        right = jnp.where(sublane == j, pivot_right, right - column * pivot_right)
    out[0:vectors] = right
    out[vectors : 2 * vectors] = pltpu.roll(wide, states - vectors, 1)
    out[2 * vectors : 3 * vectors] = jnp.broadcast_to(diagonal, (vectors, states))


def grams(mine, theirs, block, sigma_block, sigma_own, gram):
    targets, vectors, states = block.shape
    own_src = lax.axis_index("src")
    sigma_block[...] = mine[...] + theirs[...]
    sigma_own[0] = sigma_block[own_src]
    sigmas = lanes_of(sigma_block)
    both = jnp.concatenate([lanes_of(block), sigmas], axis=0)
    small = contract(sigmas, both)
    gram[...] = jnp.concatenate(
        [small, jnp.zeros((vectors, states - 2 * vectors), jnp.float32)], axis=1
    )


def finish(mine, theirs, solved, sigma_own, residual, norms):
    vectors, states = mine.shape
    gram = mine[...] + theirs[...]
    lane = lax.broadcasted_iota(jnp.int32, (vectors, states), 1)
    sublane = lax.broadcasted_iota(jnp.int32, (vectors, states), 0)
    left = sigma_own[0]
    mixing = jnp.zeros((vectors, states), jnp.float32)
    for j in range(vectors):
        column = gram[:, j : j + 1]
        left = left - column * solved[j : j + 1, :]
        mixing = mixing + column * solved[vectors + j : vectors + j + 1, :]
    residual[0] = left
    terms = jnp.where(lane == sublane + vectors, gram, 0.0) - jnp.where(
        lane < vectors, gram * mixing, 0.0
    )
    totals = jnp.sum(terms, axis=1, keepdims=True)
    column = jnp.sqrt(totals / solved[2 * vectors : 3 * vectors, :])
    norms[...] = jnp.sum(
        jnp.where(lane == sublane, column, 0.0), axis=0, keepdims=True
    )


def shards(trial_vectors, couplings, neighbours, live_slots, energies):
    vectors, _, states = trial_vectors.shape
    targets = couplings.shape[0]
    src_count, tgt_count = lax.axis_size("src"), lax.axis_size("tgt")
    f32 = jnp.float32
    params = pltpu.CompilerParams(vmem_limit_bytes=LIMIT)

    def call(body, out_shape, in_specs, out_specs, flops, moved):
        return pl.pallas_call(
            body,
            out_shape=out_shape,
            in_specs=in_specs,
            out_specs=out_specs,
            compiler_params=params,
            cost_estimate=pl.CostEstimate(
                flops=flops, bytes_accessed=moved, transcendentals=0
            ),
        )

    def shape(*dims):
        return jax.ShapeDtypeStruct(dims, f32)

    table = jnp.transpose(trial_vectors, (1, 0, 2))
    order = []
    for bit in reversed(bits_of(src_count)):
        table = jnp.concatenate([table, exchange(table, "src", bit)], axis=0)
        order.append(bit)
    for bit in reversed(bits_of(tgt_count)):
        table = jnp.concatenate([table, exchange(table, "tgt", bit)], axis=0)
        order.append(bit * src_count)

    partial, block = call(
        functools.partial(products, order),
        (shape(targets, vectors, states),) * 2,
        [VMEM, VMEM, SMEM, SMEM, VMEM],
        [VMEM, VMEM],
        2 * couplings.size * vectors,
        4 * couplings.size,
    )(table, couplings, neighbours, live_slots, energies)
    solved = call(
        invert, shape(3 * vectors, states), [VMEM], VMEM, 10**6, 4 * table.size
    )(table)

    for bit in bits_of(src_count):
        theirs = exchange(partial, "src", bit)
        if 2 * bit < src_count:
            partial = partial + theirs
    _, sigma_own, gram = call(
        grams,
        (shape(targets, vectors, states), shape(1, vectors, states), shape(vectors, states)),
        [VMEM] * 3,
        [VMEM] * 3,
        10**6,
        12 * partial.size,
    )(partial, theirs, block)

    for bit in reversed(bits_of(tgt_count)):
        theirs = exchange(gram, "tgt", bit)
        if bit > 1:
            gram = gram + theirs
    residual, norms = call(
        finish,
        (shape(1, vectors, states), shape(1, states)),
        [VMEM] * 4,
        [VMEM] * 2,
        10**4,
        10**5,
    )(gram, theirs, solved, sigma_own)
    back = lambda x: jnp.transpose(x, (1, 0, 2))
    return (back(sigma_own), back(residual), norms[0, :vectors])


def solution(mesh):
    return jax.shard_map(
        shards,
        mesh=mesh,
        in_specs=(
            P(None, ("tgt", "src"), None),
            P("tgt", "src", None, None),
            P("tgt", "src"),
            P("tgt", "src"),
            P(("tgt", "src"), None),
        ),
        out_specs=(P(None, ("tgt", "src"), None), P(None, ("tgt", "src"), None), P()),
        check_vma=False,
    )
```

time: 125 us -> 42 us (0.34); the launches traced: 123 us -> 41.8 us
  blocking collectives: 108 us -> 0 us
  starting transfers between devices: 2.57 us -> 18.3 us
  waiting for transfers between devices: 0.79 us -> 15.2 us
  other arithmetic: 4.12 us -> 0.02 us
  Pallas kernels: 0 us -> 3.85 us
  matrix products: 2.34 us -> 0 us
    psum x1 -> x0, blocking collectives: 38.7 us -> none  [shards(): lax.psum((projected, metric, squares), ('tgt', 'src'))]
    unnamed x1 -> x0, blocking collectives: 37 us -> none
    all_gather x1 -> x0, blocking collectives: 32.5 us -> none  [shards(): source_block = lax.all_gather(trial_vectors, 'src', axis=1, tiled=True)]
    ppermute x2 -> x10, starting transfers between devices: 2.57 us -> 18.3 us  [exchange(): return lax.ppermute(x, axis, [(i, i ^ bit) for i in range(count)])]
    ppermute x2 -> x10, waiting for transfers between devices: 0.79 us -> 15.2 us  [exchange(): return lax.ppermute(x, axis, [(i, i ^ bit) for i in range(count)])]
    pallas_call x0 -> x4, Pallas kernels: none -> 3.85 us  [the longest x1 1.6 us: shards(): call(functools.partial(products, order), (shape(targets, vectors, states)...]
    another operation x5 -> x0, other arithmetic: 2.67 us -> none  [the longest x3 1.39 us: shards(): factor = jnp.linalg.cholesky(metric)]
    dot_general x4 -> x0, matrix products: 2.01 us -> none  [the longest x1 0.95 us: shards(): jnp.einsum('inab,kinb->kia', couplings, fetched, precision=lax.Precision....]
  transfers between devices with their start and end apart: 2 -> 10, of which waited for: 1 -> 10; matrix products, arithmetic and copies ran while one was open for 1% -> 2% of each run, Pallas kernels for 0% -> 2%
where the time goes in v1:
time: 42 us; the launch traced here: 41.8 us
  starting transfers between devices  18.3 us (44%)
  waiting for transfers between devices  15.2 us (36%)
  Pallas kernels  3.85 us (9%)
  local copies, waits for them, and re-layouts  3.71 us (9%)
  between operations  0.68 us (2%)
    ppermute x10, starting transfers between devices, exchange(): return lax.ppermute(x, axis, [(i, i ^ bit) for i in range(count)])  18.3 us
    ppermute x10, waiting for transfers between devices, exchange(): return lax.ppermute(x, axis, [(i, i ^ bit) for i in range(count)])  15.2 us
    unnamed x18, local copies, waits for them, and re-layouts  3.18 us
    pallas_call x1, Pallas kernels, shards(): call(functools.partial(products, order), (shape(targets, vectors, states)...  1.6 us
    pallas_call x1, Pallas kernels, shards(): call(invert, shape(3 * vectors, states), [VMEM], VMEM, 10 ** 6, 4 * table...  0.95 us
  transfers between devices with their start and end apart: 10, of which 10 were waited for; matrix products, arithmetic and copies ran while one was open for 2% of the time, Pallas kernels for 2%

profile of v1, /device:TPU:0, one launch (start us, length us, event | category | flops | bytes accessed | tf_op | source)
XLA Modules:
  0.0 41.8 jit_solution(17805184688360203490)
XLA Ops:
  0.6 4.1 %collective-permute-start = (f32[1,8,128]{2,1,0:T(8,128)}, f32[1,8,128]{2,1,0:T(8,128)S(1)}, u32[]{:S(2)}, u32[]{:S(2)}) collective-permute-start(f32[1,8,128]{2,1,0:T(8,128)} %bitcast.13), channel_id=1, source_target_pairs={{0,4},{1,5},{2,6},{3,7},{4,0},{5,1},{6,2},{7,3},{8,12},{9,13},{10,... | collective-permute-start | bytes 12296 | tf_op jit(solution)/shard_map/ppermute | solution.py:18
  4.7 0.0 copy-start.3
  4.7 0.8 %constant_dynamic-update-slice_fusion.4 = (f32[16,8,128]{2,1,0:T(8,128)S(1)}, f32[32,8,128]{2,1,0:T(8,128)S(1)}) fusion(f32[1,8,128]{2,1,0:T(8,128)} %bitcast.14), kind=kLoop, calls=%fused_computation.5 | loop fusion | bytes 12288
  5.5 1.0 %collective-permute-done = f32[1,8,128]{2,1,0:T(8,128)S(1)} collective-permute-done((f32[1,8,128]{2,1,0:T(8,128)}, f32[1,8,128]{2,1,0:T(8,128)S(1)}, u32[]{:S(2)}, u32[]{:S(2)}) %collective-permute-start) | collective-permute-done | bytes 4128 | tf_op jit(solution)/shard_map/ppermute | solution.py:18
  6.5 0.0 copy-done.3
  6.5 1.9 %collective-permute-start.1 = (f32[2,8,128]{2,1,0:T(8,128)S(1)}, f32[2,8,128]{2,1,0:T(8,128)S(1)}, u32[]{:S(2)}, u32[]{:S(2)}) collective-permute-start(f32[2,8,128]{2,1,0:T(8,128)S(1)} %pad_maximum_fusion.2), channel_id=1, source_target_pairs={{0,2},{1,3},{2,0},{3,1},{4,6},{5,7},{6,4},{7,5},{8,10},{9,11},{10,... | collective-permute-start | bytes 24584 | tf_op jit(solution)/shard_map/ppermute | solution.py:18
  8.4 1.7 %collective-permute-done.1 = f32[2,8,128]{2,1,0:T(8,128)S(1)} collective-permute-done((f32[2,8,128]{2,1,0:T(8,128)S(1)}, f32[2,8,128]{2,1,0:T(8,128)S(1)}, u32[]{:S(2)}, u32[]{:S(2)}) %collective-permute-start.1) | collective-permute-done | bytes 8224 | tf_op jit(solution)/shard_map/ppermute | solution.py:18
  10.2 1.8 %collective-permute-start.2 = (f32[4,8,128]{2,1,0:T(8,128)S(1)}, f32[4,8,128]{2,1,0:T(8,128)S(1)}, u32[]{:S(2)}, u32[]{:S(2)}) collective-permute-start(f32[4,8,128]{2,1,0:T(8,128)S(1)} %pad_maximum_fusion.1), channel_id=1, source_target_pairs={{0,1},{1,0},{2,3},{3,2},{4,5},{5,4},{6,7},{7,6},{8,9},{9,8},{10,11... | collective-permute-start | bytes 49160 | tf_op jit(solution)/shard_map/ppermute | solution.py:18
  12.0 1.9 %collective-permute-done.2 = f32[4,8,128]{2,1,0:T(8,128)S(1)} collective-permute-done((f32[4,8,128]{2,1,0:T(8,128)S(1)}, f32[4,8,128]{2,1,0:T(8,128)S(1)}, u32[]{:S(2)}, u32[]{:S(2)}) %collective-permute-start.2) | collective-permute-done | bytes 16416 | tf_op jit(solution)/shard_map/ppermute | solution.py:18
  13.9 1.9 %collective-permute-start.3 = (f32[8,8,128]{2,1,0:T(8,128)S(1)}, f32[8,8,128]{2,1,0:T(8,128)S(1)}, u32[]{:S(2)}, u32[]{:S(2)}) collective-permute-start(f32[8,8,128]{2,1,0:T(8,128)S(1)} %pad_maximum_fusion), channel_id=1, source_target_pairs={{0,16},{8,24},{16,0},{24,8},{1,17},{9,25},{17,1},{25,9},{2,18},{10... | collective-permute-start | bytes 98312 | tf_op jit(solution)/shard_map/ppermute | solution.py:18
  15.8 2.1 %collective-permute-done.3 = f32[8,8,128]{2,1,0:T(8,128)S(1)} collective-permute-done((f32[8,8,128]{2,1,0:T(8,128)S(1)}, f32[8,8,128]{2,1,0:T(8,128)S(1)}, u32[]{:S(2)}, u32[]{:S(2)}) %collective-permute-start.3) | collective-permute-done | bytes 32800 | tf_op jit(solution)/shard_map/ppermute | solution.py:18
  17.9 0.0 copy-start.4
  17.9 0.0 copy-start.5
  17.9 0.1 collective-permute-start.4
  17.9 0.6 %copy-done.4 = s32[8,1]{0,1:T(1,128)S(1)} copy-done((s32[8,1]{0,1:T(1,128)S(1)}, s32[8,1]{0,1:T(1,128)}, u32[]{:S(2)}) %copy-start.4) | copy-done | bytes 56
  18.5 0.1 copy.8.neighbours
  18.6 0.0 copy-done.5
  18.6 0.1 copy.9.live
  18.7 0.5 %collective-permute-done.4 = f32[16,8,128]{2,1,0:T(8,128)S(1)} collective-permute-done((f32[16,8,128]{2,1,0:T(8,128)S(1)}, f32[16,8,128]{2,1,0:T(8,128)S(1)}, u32[]{:S(2)}, u32[]{:S(2)}) %collective-permute-start.4) | collective-permute-done | bytes 65568 | tf_op jit(solution)/shard_map/ppermute | solution.py:18
  19.2 0.0 copy-start.2
  19.2 0.6 %copy-done.2 = f32[1,128]{1,0:T(1,128)S(1)} copy-done((f32[1,128]{1,0:T(1,128)S(1)}, f32[1,128]{1,0:T(1,128)}, u32[]{:S(2)}) %copy-start.2) | copy-done | bytes 536
  19.8 0.0 copy-start
  19.9 1.0 %copy-done = f32[8,1,128,128]{3,2,1,0:T(8,128)S(1)} copy-done((f32[8,1,128,128]{3,2,1,0:T(8,128)S(1)}, f32[8,1,128,128]{3,2,1,0:T(8,128)}, u32[]{:S(2)}) %copy-start) | copy-done | bytes 524312
  20.9 1.6 %shard_map.76 = (f32[8,8,128]{2,1,0:T(8,128)S(1)}, f32[8,8,128]{2,1,0:T(8,128)S(1)}) custom-call(f32[32,8,128]{2,1,0:T(8,128)S(1)} %constant_dynamic-update-slice_fusion.5.table, f32[8,1,128,128]{3,2,1,0:T(8,128)S(1)} %copy-done, s32[8,1]{1,0:T(8,128)S(1)} %copy.8.neighbours, s32[8,1]{1,0:T(8,128)S(1)} %copy.9.live, f32[1,128]{1,0:T(1,128)S(1)} %copy-done.2), custom_call_target="tpu_custom_call" | custom-call | flops 2097152 | bytes 524288 | tf_op jit(solution)/shard_map/pallas_call | solution.py:166
  22.5 1.9 %collective-permute-start.5 = (f32[8,8,128]{2,1,0:T(8,128)S(1)}, f32[8,8,128]{2,1,0:T(8,128)S(1)}, u32[]{:S(2)}, u32[]{:S(2)}) collective-permute-start(f32[8,8,128]{2,1,0:T(8,128)S(1)} %get-tuple-element.9), channel_id=1, source_target_pairs={{0,1},{1,0},{2,3},{3,2},{4,5},{5,4},{6,7},{7,6},{8,9},{9,8},{10,11... | collective-permute-start | bytes 98312 | tf_op jit(solution)/shard_map/ppermute | solution.py:18
  24.3 2.1 %collective-permute-done.5 = f32[8,8,128]{2,1,0:T(8,128)S(1)} collective-permute-done((f32[8,8,128]{2,1,0:T(8,128)S(1)}, f32[8,8,128]{2,1,0:T(8,128)S(1)}, u32[]{:S(2)}, u32[]{:S(2)}) %collective-permute-start.5) | collective-permute-done | bytes 32800 | tf_op jit(solution)/shard_map/ppermute | solution.py:18
  26.4 1.9 %collective-permute-start.6 = (f32[8,8,128]{2,1,0:T(8,128)S(1)}, f32[8,8,128]{2,1,0:T(8,128)S(1)}, u32[]{:S(2)}, u32[]{:S(2)}) collective-permute-start(f32[8,8,128]{2,1,0:T(8,128)S(1)} %add.9), channel_id=1, source_target_pairs={{0,2},{1,3},{2,0},{3,1},{4,6},{5,7},{6,4},{7,5},{8,10},{9,11},{10,... | collective-permute-start | bytes 98312 | tf_op jit(solution)/shard_map/ppermute | solution.py:18
  28.4 2.0 %collective-permute-done.6 = f32[8,8,128]{2,1,0:T(8,128)S(1)} collective-permute-done((f32[8,8,128]{2,1,0:T(8,128)S(1)}, f32[8,8,128]{2,1,0:T(8,128)S(1)}, u32[]{:S(2)}, u32[]{:S(2)}) %collective-permute-start.6) | collective-permute-done | bytes 32800 | tf_op jit(solution)/shard_map/ppermute | solution.py:18
  30.4 2.9 %collective-permute-start.7 = (f32[8,8,128]{2,1,0:T(8,128)S(1)}, f32[8,8,128]{2,1,0:T(8,128)S(1)}, u32[]{:S(2)}, u32[]{:S(2)}) collective-permute-start(f32[8,8,128]{2,1,0:T(8,128)S(1)} %add.10.mine), channel_id=1, source_target_pairs={{0,4},{1,5},{2,6},{3,7},{4,0},{5,1},{6,2},{7,3},{8,12},{9,13},{10,... | collective-permute-start | bytes 98312 | tf_op jit(solution)/shard_map/ppermute | solution.py:18
  33.3 1.9 %collective-permute-done.7.theirs = f32[8,8,128]{2,1,0:T(8,128)S(1)} collective-permute-done((f32[8,8,128]{2,1,0:T(8,128)S(1)}, f32[8,8,128]{2,1,0:T(8,128)S(1)}, u32[]{:S(2)}, u32[]{:S(2)}) %collective-permute-start.7) | collective-permute-done | bytes 32800 | tf_op jit(solution)/shard_map/ppermute | solution.py:18
  35.2 0.6 %shard_map.77 = (f32[8,8,128]{2,1,0:T(8,128)}, f32[1,8,128]{2,1,0:T(8,128)}, f32[8,128]{1,0:T(8,128)S(1)}) custom-call(f32[8,8,128]{2,1,0:T(8,128)S(1)} %add.10.mine, f32[8,8,128]{2,1,0:T(8,128)S(1)} %collective-permute-done.7.theirs, f32[8,8,128]{2,1,0:T(8,128)S(1)} %get-tuple-element.10.block), custom_call_target="tpu_custom_call" | custom-call | flops 1000000 | bytes 98304 | tf_op jit(solution)/shard_map/pallas_call | solution.py:182
  35.8 1.9 %collective-permute-start.8 = (f32[8,128]{1,0:T(8,128)S(1)}, f32[8,128]{1,0:T(8,128)S(1)}, u32[]{:S(2)}, u32[]{:S(2)}) collective-permute-start(f32[8,128]{1,0:T(8,128)S(1)} %get-tuple-element.12), channel_id=1, source_target_pairs={{0,16},{8,24},{16,0},{24,8},{1,17},{9,25},{17,1},{25,9},{2,18},{10... | collective-permute-start | bytes 12296 | tf_op jit(solution)/shard_map/ppermute | solution.py:18
  37.7 1.8 %collective-permute-done.8 = f32[8,128]{1,0:T(8,128)S(1)} collective-permute-done((f32[8,128]{1,0:T(8,128)S(1)}, f32[8,128]{1,0:T(8,128)S(1)}, u32[]{:S(2)}, u32[]{:S(2)}) %collective-permute-start.8) | collective-permute-done | bytes 4128 | tf_op jit(solution)/shard_map/ppermute | solution.py:18
  39.4 0.0 collective-permute-start.9
  39.4 0.0 copy-start.1
  39.4 0.9 %shard_map.78.solved = f32[24,128]{1,0:T(8,128)S(1)} custom-call(f32[32,8,128]{2,1,0:T(8,128)S(1)} %constant_dynamic-update-slice_fusion.5.table), custom_call_target="tpu_custom_call" | custom-call | flops 1000000 | bytes 131072 | tf_op jit(solution)/shard_map/pallas_call | solution.py:174
  40.4 0.2 collective-permute-done.9.theirs
  40.6 0.0 copy-done.1
  40.6 0.7 %shard_map.79 = (f32[1,8,128]{2,1,0:T(8,128)}, f32[1,128]{1,0:T(1,128)S(1)}) custom-call(f32[8,128]{1,0:T(8,128)S(1)} %add.11.mine, f32[8,128]{1,0:T(8,128)S(1)} %collective-permute-done.9.theirs, f32[24,128]{1,0:T(8,128)S(1)} %shard_map.78.solved, f32[1,8,128]{2,1,0:T(8,128)S(1)} %copy-done.1), custom_call_target="tpu_custom_call" | custom-call | flops 10000 | bytes 100000 | tf_op jit(solution)/shard_map/pallas_call | solution.py:195
  41.3 0.5 %slice_bitcast_fusion = f32[8]{0:T(128)} fusion(f32[1,128]{1,0:T(1,128)S(1)} %get-tuple-element.14), kind=kLoop, calls=%fused_computation.14 | loop fusion | bytes 64 | tf_op jit(solution)/shard_map/squeeze | solution.py:204
  (11 shorter events, 0.0 us)
Async XLA Ops:
  0.6 5.9 %collective-permute-start = (f32[1,8,128]{2,1,0:T(8,128)}, f32[1,8,128]{2,1,0:T(8,128)S(1)}, u32[]{:S(2)}, u32[]{:S(2)}) collective-permute-start(f32[1,8,128]{2,1,0:T(8,128)} %bitcast.13), channel_id=1, source_target_pairs={{0,4},{1,5},{2,6},{3,7},{4,0},{5,1},{6,2},{7,3},{8,12},{9,13},{10,... | collective-permute-start | bytes 12296 | tf_op jit(solution)/shard_map/ppermute | solution.py:18
  4.7 1.8 %copy-start.3 = (f32[8,1,128]{2,1,0:T(1,128)S(1)}, f32[8,1,128]{2,1,0:T(1,128)}, u32[]{:S(2)}) copy-start(f32[8,1,128]{2,1,0:T(1,128)} %param.5) | copy-start | bytes 12292
  6.5 3.7 %collective-permute-start.1 = (f32[2,8,128]{2,1,0:T(8,128)S(1)}, f32[2,8,128]{2,1,0:T(8,128)S(1)}, u32[]{:S(2)}, u32[]{:S(2)}) collective-permute-start(f32[2,8,128]{2,1,0:T(8,128)S(1)} %pad_maximum_fusion.2), channel_id=1, source_target_pairs={{0,2},{1,3},{2,0},{3,1},{4,6},{5,7},{6,4},{7,5},{8,10},{9,11},{10,... | collective-permute-start | bytes 24584 | tf_op jit(solution)/shard_map/ppermute | solution.py:18
  10.2 3.7 %collective-permute-start.2 = (f32[4,8,128]{2,1,0:T(8,128)S(1)}, f32[4,8,128]{2,1,0:T(8,128)S(1)}, u32[]{:S(2)}, u32[]{:S(2)}) collective-permute-start(f32[4,8,128]{2,1,0:T(8,128)S(1)} %pad_maximum_fusion.1), channel_id=1, source_target_pairs={{0,1},{1,0},{2,3},{3,2},{4,5},{5,4},{6,7},{7,6},{8,9},{9,8},{10,11... | collective-permute-start | bytes 49160 | tf_op jit(solution)/shard_map/ppermute | solution.py:18
  13.9 3.9 %collective-permute-start.3 = (f32[8,8,128]{2,1,0:T(8,128)S(1)}, f32[8,8,128]{2,1,0:T(8,128)S(1)}, u32[]{:S(2)}, u32[]{:S(2)}) collective-permute-start(f32[8,8,128]{2,1,0:T(8,128)S(1)} %pad_maximum_fusion), channel_id=1, source_target_pairs={{0,16},{8,24},{16,0},{24,8},{1,17},{9,25},{17,1},{25,9},{2,18},{10... | collective-permute-start | bytes 98312 | tf_op jit(solution)/shard_map/ppermute | solution.py:18
  17.9 0.7 %copy-start.4 = (s32[8,1]{0,1:T(1,128)S(1)}, s32[8,1]{0,1:T(1,128)}, u32[]{:S(2)}) copy-start(s32[8,1]{0,1:T(1,128)} %param.7) | copy-start | bytes 100
  17.9 0.7 %copy-start.5 = (s32[8,1]{0,1:T(1,128)S(1)}, s32[8,1]{0,1:T(1,128)}, u32[]{:S(2)}) copy-start(s32[8,1]{0,1:T(1,128)} %param.8) | copy-start | bytes 100
  17.9 1.3 %collective-permute-start.4 = (f32[16,8,128]{2,1,0:T(8,128)S(1)}, f32[16,8,128]{2,1,0:T(8,128)S(1)}, u32[]{:S(2)}, u32[]{:S(2)}) collective-permute-start(f32[16,8,128]{2,1,0:T(8,128)S(1)} %get-tuple-element.18), channel_id=1, source_target_pairs={{0,8},{8,0},{16,24},{24,16},{1,9},{9,1},{17,25},{25,17},{2,10},{10... | collective-permute-start | bytes 196616 | tf_op jit(solution)/shard_map/ppermute | solution.py:18
  19.2 0.7 %copy-start.2 = (f32[1,128]{1,0:T(1,128)S(1)}, f32[1,128]{1,0:T(1,128)}, u32[]{:S(2)}) copy-start(f32[1,128]{1,0:T(1,128)} %energies.1) | copy-start | bytes 1540
  19.8 1.0 %copy-start = (f32[8,1,128,128]{3,2,1,0:T(8,128)S(1)}, f32[8,1,128,128]{3,2,1,0:T(8,128)}, u32[]{:S(2)}) copy-start(f32[8,1,128,128]{3,2,1,0:T(8,128)} %couplings.1) | copy-start | bytes 1572868
  22.5 3.9 %collective-permute-start.5 = (f32[8,8,128]{2,1,0:T(8,128)S(1)}, f32[8,8,128]{2,1,0:T(8,128)S(1)}, u32[]{:S(2)}, u32[]{:S(2)}) collective-permute-start(f32[8,8,128]{2,1,0:T(8,128)S(1)} %get-tuple-element.9), channel_id=1, source_target_pairs={{0,1},{1,0},{2,3},{3,2},{4,5},{5,4},{6,7},{7,6},{8,9},{9,8},{10,11... | collective-permute-start | bytes 98312 | tf_op jit(solution)/shard_map/ppermute | solution.py:18
  26.4 3.9 %collective-permute-start.6 = (f32[8,8,128]{2,1,0:T(8,128)S(1)}, f32[8,8,128]{2,1,0:T(8,128)S(1)}, u32[]{:S(2)}, u32[]{:S(2)}) collective-permute-start(f32[8,8,128]{2,1,0:T(8,128)S(1)} %add.9), channel_id=1, source_target_pairs={{0,2},{1,3},{2,0},{3,1},{4,6},{5,7},{6,4},{7,5},{8,10},{9,11},{10,... | collective-permute-start | bytes 98312 | tf_op jit(solution)/shard_map/ppermute | solution.py:18
  30.4 4.8 %collective-permute-start.7 = (f32[8,8,128]{2,1,0:T(8,128)S(1)}, f32[8,8,128]{2,1,0:T(8,128)S(1)}, u32[]{:S(2)}, u32[]{:S(2)}) collective-permute-start(f32[8,8,128]{2,1,0:T(8,128)S(1)} %add.10.mine), channel_id=1, source_target_pairs={{0,4},{1,5},{2,6},{3,7},{4,0},{5,1},{6,2},{7,3},{8,12},{9,13},{10,... | collective-permute-start | bytes 98312 | tf_op jit(solution)/shard_map/ppermute | solution.py:18
  35.8 3.6 %collective-permute-start.8 = (f32[8,128]{1,0:T(8,128)S(1)}, f32[8,128]{1,0:T(8,128)S(1)}, u32[]{:S(2)}, u32[]{:S(2)}) collective-permute-start(f32[8,128]{1,0:T(8,128)S(1)} %get-tuple-element.12), channel_id=1, source_target_pairs={{0,16},{8,24},{16,0},{24,8},{1,17},{9,25},{17,1},{25,9},{2,18},{10... | collective-permute-start | bytes 12296 | tf_op jit(solution)/shard_map/ppermute | solution.py:18
  39.4 1.2 %collective-permute-start.9 = (f32[8,128]{1,0:T(8,128)S(1)}, f32[8,128]{1,0:T(8,128)S(1)}, u32[]{:S(2)}, u32[]{:S(2)}) collective-permute-start(f32[8,128]{1,0:T(8,128)S(1)} %add.11.mine), channel_id=1, source_target_pairs={{0,8},{8,0},{16,24},{24,16},{1,9},{9,1},{17,25},{25,17},{2,10},{10... | collective-permute-start | bytes 12296 | tf_op jit(solution)/shard_map/ppermute | solution.py:18
  39.4 1.2 %copy-start.1 = (f32[1,8,128]{2,1,0:T(8,128)S(1)}, f32[1,8,128]{2,1,0:T(8,128)}, u32[]{:S(2)}) copy-start(f32[1,8,128]{2,1,0:T(8,128)} %get-tuple-element.11.sigma_own) | copy-start | bytes 12292

commit v2 on v1

v2 whole, which is shorter than its diff:
```python
import jax
import jax.numpy as jnp
from jax import lax
from jax.experimental import pallas as pl
from jax.experimental.pallas import tpu as pltpu
from jax.sharding import PartitionSpec as P

VMEM = pl.BlockSpec(memory_space=pltpu.VMEM)
SMEM = pl.BlockSpec(memory_space=pltpu.SMEM)
LIMIT = 24 * 2**20


def exchange(x, axis, bit):
    count = lax.axis_size(axis)
    return lax.ppermute(x, axis, [(i, i ^ bit) for i in range(count)])


def bits_of(count):
    return [1 << n for n in range(count.bit_length() - 1)]


def split(x):
    high = x.astype(jnp.bfloat16)
    return high, (x - high.astype(jnp.float32)).astype(jnp.bfloat16)


def spread(row, copies):
    for i in range(copies.shape[0]):
        copies[i] = row[0]


def prepare(couplings, live, neighbours, energies, row, high, low, sources, diagonal):
    targets, slots = couplings.shape[0], couplings.shape[1]
    for i in range(targets):
        for n in range(slots):
            weight = live[i * slots + n].astype(jnp.float32)
            high[i, n], low[i, n] = split(couplings[i, n] * weight)
    sources[...] = neighbours[...]
    diagonal[...] = row[0] * energies[...]


def times(left, right):
    return lax.dot_general(
        left, right, (((1,), (1,)), ((), ())), preferred_element_type=jnp.float32
    )


def products(table, high, low, sources, diagonal, partial):
    targets, slots = high.shape[0], high.shape[1]
    vectors = table.shape[1]
    own_src = lax.axis_index("src")
    at = sources[...]
    for i in range(targets):
        total = None
        for n in range(slots):
            row = jnp.concatenate(split(table[at[i, n]]), axis=0)
            term = times(row, high[i, n]) + times(row, low[i, n])
            total = term if total is None else total + term
        partial[i] = total[:vectors] + total[vectors:]
    partial[own_src] = partial[own_src] + diagonal[...]


def contract(left, right):
    return lax.dot_general(
        left,
        right,
        (((1,), (1,)), ((), ())),
        precision=lax.Precision.HIGHEST,
        preferred_element_type=jnp.float32,
    )


def invert(table, out):
    rows, vectors, states = table.shape
    metric = jnp.zeros((vectors, vectors), jnp.float32)
    step = 32
    for r in range(0, rows, step):
        part = jnp.concatenate([table[i] for i in range(r, min(r + step, rows))], axis=1)
        metric = metric + contract(part, part)
    eye = (
        lax.broadcasted_iota(jnp.int32, (vectors, vectors), 0)
        == lax.broadcasted_iota(jnp.int32, (vectors, vectors), 1)
    )
    diagonal = jnp.sum(jnp.where(eye, metric, 0.0), axis=1, keepdims=True)
    sublane = lax.broadcasted_iota(jnp.int32, (vectors, states), 0)
    right = table[lax.axis_index("tgt") * lax.axis_size("src") + lax.axis_index("src")]
    wide = jnp.concatenate(
        [metric, jnp.where(eye, 1.0, 0.0), jnp.zeros((vectors, states - 2 * vectors), jnp.float32)],
        axis=1,
    )
    for j in range(vectors):
        column = wide[:, j : j + 1]
        inverse = 1.0 / wide[j : j + 1, j : j + 1]
        pivot = wide[j : j + 1, :] * inverse
        pivot_right = right[j : j + 1, :] * inverse
        wide = jnp.where(sublane == j, pivot, wide - column * pivot)
        right = jnp.where(sublane == j, pivot_right, right - column * pivot_right)
    out[0:vectors] = right
    out[vectors : 2 * vectors] = pltpu.roll(wide, states - vectors, 1)
    out[2 * vectors : 3 * vectors] = jnp.broadcast_to(diagonal, (vectors, states))


def grams(mine, theirs, table, own, gram, sigmas):
    targets, vectors, states = mine.shape
    first = lax.axis_index("tgt") * targets
    sigmas[...] = mine[...] + theirs[...]
    own[...] = sigmas[lax.axis_index("src")]
    block = jnp.concatenate([table[first + i] for i in range(targets)], axis=1)
    wide = jnp.concatenate([sigmas[i] for i in range(targets)], axis=1)
    small = contract(wide, jnp.concatenate([block, wide], axis=0))
    gram[...] = jnp.concatenate(
        [small, jnp.zeros((vectors, states - 2 * vectors), jnp.float32)], axis=1
    )


def finish(mine, theirs, solved, own, sigma, residual, norms):
    vectors, states = mine.shape
    gram = mine[...] + theirs[...]
    lane = lax.broadcasted_iota(jnp.int32, (vectors, states), 1)
    sublane = lax.broadcasted_iota(jnp.int32, (vectors, states), 0)
    left = own[...]
    sigma[0] = left
    mixing = jnp.zeros((vectors, states), jnp.float32)
    for j in range(vectors):
        column = gram[:, j : j + 1]
        left = left - column * solved[j : j + 1, :]
        mixing = mixing + column * solved[vectors + j : vectors + j + 1, :]
    residual[0] = left
    terms = jnp.where(lane == sublane + vectors, gram, 0.0) - jnp.where(
        lane < vectors, gram * mixing, 0.0
    )
    totals = jnp.sum(terms, axis=1, keepdims=True)
    column = jnp.sqrt(totals / solved[2 * vectors : 3 * vectors, :])
    norms[...] = jnp.sum(jnp.where(lane == sublane, column, 0.0), axis=0)[:vectors]


def shards(trial_vectors, couplings, neighbours, live_slots, energies):
    vectors, _, states = trial_vectors.shape
    targets = couplings.shape[0]
    src_count, tgt_count = lax.axis_size("src"), lax.axis_size("tgt")
    params = pltpu.CompilerParams(vmem_limit_bytes=LIMIT)

    def call(body, outs, in_specs, flops, moved, scratch=()):
        return pl.pallas_call(
            body,
            out_shape=outs,
            in_specs=in_specs,
            out_specs=jax.tree.map(lambda _: VMEM, outs),
            scratch_shapes=scratch,
            compiler_params=params,
            cost_estimate=pl.CostEstimate(
                flops=flops, bytes_accessed=moved, transcendentals=0
            ),
        )

    def shape(*dims, dtype=jnp.float32):
        return jax.ShapeDtypeStruct(dims, dtype)

    size = couplings.size
    row = jnp.transpose(trial_vectors, (1, 0, 2))
    copies = call(
        spread, shape(src_count * tgt_count, vectors, states), [VMEM], 0, 10**5
    )(row)
    high, low, sources, diagonal = call(
        prepare,
        (
            shape(*couplings.shape, dtype=jnp.bfloat16),
            shape(*couplings.shape, dtype=jnp.bfloat16),
            shape(*neighbours.shape, dtype=jnp.int32),
            shape(vectors, states),
        ),
        [VMEM, SMEM, VMEM, VMEM, VMEM],
        4 * size,
        8 * size,
    )(couplings, live_slots.reshape(-1), neighbours, energies, row)
    table = lax.all_to_all(copies, ("tgt", "src"), 0, 0, tiled=True)
    partial = call(
        products, shape(targets, vectors, states), [VMEM] * 5, 2 * size * vectors, 4 * size
    )(table, high, low, sources, diagonal)
    solved = call(invert, shape(3 * vectors, states), [VMEM], 10**6, 4 * table.size)(table)

    for bit in bits_of(src_count):
        theirs = exchange(partial, "src", bit)
        if 2 * bit < src_count:
            partial = partial + theirs
    own, gram = call(
        grams,
        (shape(vectors, states), shape(vectors, states)),
        [VMEM] * 3,
        10**6,
        12 * partial.size,
        [pltpu.VMEM((targets, vectors, states), jnp.float32)],
    )(partial, theirs, table)

    for bit in reversed(bits_of(tgt_count)):
        theirs = exchange(gram, "tgt", bit)
        if bit > 1:
            gram = gram + theirs
    sigma, residual, norms = call(
        finish,
        (shape(1, vectors, states), shape(1, vectors, states), shape(vectors)),
        [VMEM] * 4,
        10**4,
        10**5,
    )(gram, theirs, solved, own)
    return (jnp.transpose(sigma, (1, 0, 2)), jnp.transpose(residual, (1, 0, 2)), norms)


def solution(mesh):
    return jax.shard_map(
        shards,
        mesh=mesh,
        in_specs=(
            P(None, ("tgt", "src"), None),
            P("tgt", "src", None, None),
            P("tgt", "src"),
            P("tgt", "src"),
            P(("tgt", "src"), None),
        ),
        out_specs=(P(None, ("tgt", "src"), None), P(None, ("tgt", "src"), None), P()),
        check_vma=False,
    )
```

time: 42 us -> 36 us (0.86)
  starting transfers between devices: 18.3 us -> 12.3 us
  waiting for transfers between devices: 15.2 us -> 16.8 us
  local copies, waits for them, and re-layouts: 3.71 us -> 2.48 us
    ppermute x10 -> x5, starting transfers between devices: 18.3 us -> 4.97 us  [exchange(): return lax.ppermute(x, axis, [(i, i ^ bit) for i in range(count)])]
    all_to_all x0 -> x1, starting transfers between devices: none -> 7.3 us  [shards(): table = lax.all_to_all(copies, ('tgt', 'src'), 0, 0, tiled=True)]
    all_to_all x0 -> x1, waiting for transfers between devices: none -> 5.3 us  [shards(): table = lax.all_to_all(copies, ('tgt', 'src'), 0, 0, tiled=True)]
    ppermute x10 -> x5, waiting for transfers between devices: 15.2 us -> 11.5 us  [exchange(): return lax.ppermute(x, axis, [(i, i ^ bit) for i in range(count)])]
    unnamed x18 -> x13, local copies, waits for them, and re-layouts: 3.18 us -> 2.48 us
    squeeze x1 -> x0, local copies, waits for them, and re-layouts: 0.51 us -> none  [shards(): return (back(sigma_own), back(residual), norms[0, :vectors])]
    pallas_call x4 -> x6, Pallas kernels: 3.85 us -> 3.48 us  [the longest x1 0.95 us: shards(): call(invert, shape(3 * vectors, states), [VMEM], 10 ** 6, 4 * table.size)]
  transfers between devices with their start and end apart: 10 -> 6, of which waited for: 10 -> 6; matrix products, arithmetic and copies ran while one was open for 2% -> 0% of each run, Pallas kernels for 2% -> 4%
where the time goes in v2:
time: 36 us; the launch traced here: 35.8 us
  waiting for transfers between devices  16.8 us (47%)
  starting transfers between devices  12.3 us (34%)
  Pallas kernels  3.48 us (10%)
  local copies, waits for them, and re-layouts  2.48 us (7%)
  between operations  0.68 us (2%)
    ppermute x5, waiting for transfers between devices, exchange(): return lax.ppermute(x, axis, [(i, i ^ bit) for i in range(count)])  11.5 us
    all_to_all x1, starting transfers between devices, shards(): table = lax.all_to_all(copies, ('tgt', 'src'), 0, 0, tiled=True)  7.3 us
    all_to_all x1, waiting for transfers between devices, shards(): table = lax.all_to_all(copies, ('tgt', 'src'), 0, 0, tiled=True)  5.3 us
    ppermute x5, starting transfers between devices, exchange(): return lax.ppermute(x, axis, [(i, i ^ bit) for i in range(count)])  4.97 us
    unnamed x13, local copies, waits for them, and re-layouts  2.48 us
    pallas_call x1, Pallas kernels, shards(): call(invert, shape(3 * vectors, states), [VMEM], 10 ** 6, 4 * table.size)  0.95 us
  transfers between devices with their start and end apart: 6, of which 6 were waited for; matrix products, arithmetic and copies ran while one was open for 0% of the time, Pallas kernels for 4%

profile of v2, /device:TPU:0, one launch (start us, length us, event | category | flops | bytes accessed | tf_op | source)
XLA Modules:
  0.0 35.8 jit_solution(6665932897729472352)
XLA Ops:
  0.6 0.0 copy-start.1
  0.6 0.7 %copy-done.1 = f32[8,1,128]{2,1,0:T(1,128)S(1)} copy-done((f32[8,1,128]{2,1,0:T(1,128)S(1)}, f32[8,1,128]{2,1,0:T(1,128)}, u32[]{:S(2)}) %copy-start.1) | copy-done | bytes 4120
  1.3 0.7 %shard_map.76 = f32[32,8,128]{2,1,0:T(8,128)} custom-call(f32[1,8,128]{2,1,0:T(8,128)S(1)} %bitcast.8), custom_call_target="tpu_custom_call" | custom-call | bytes 100000 | tf_op jit(solution)/shard_map/pallas_call | solution.py:161
  2.0 0.0 copy-start.5
  2.0 7.3 %all-to-all-start = ((f32[32,8,128]{2,1,0:T(8,128)}), f32[32,8,128]{2,1,0:T(8,128)S(1)}, u32[]{:S(2)}, u32[]{:S(2)}) async-start(f32[32,8,128]{2,1,0:T(8,128)} %shard_map.76), calls=%async_computation | async-start | bytes 262144 | tf_op jit(solution)/shard_map/all_to_all | solution.py:176
  9.3 0.0 copy-done.5
  9.3 0.0 copy-start.2
  9.3 0.1 copy.8.neighbours
  9.4 0.0 copy-start.3
  9.4 0.0 copy-start.4
  9.4 0.6 %copy-done.2 = f32[8,1,128]{2,1,0:T(1,128)S(1)} copy-done((f32[8,1,128]{2,1,0:T(1,128)S(1)}, f32[8,1,128]{2,1,0:T(1,128)}, u32[]{:S(2)}) %copy-start.2) | copy-done | bytes 4120
  10.0 0.1 copy-done.3
  10.1 0.0 copy-done.4
  10.1 0.0 copy-start
  10.1 1.0 %copy-done = f32[8,1,128,128]{3,2,1,0:T(8,128)S(1)} copy-done((f32[8,1,128,128]{3,2,1,0:T(8,128)S(1)}, f32[8,1,128,128]{3,2,1,0:T(8,128)}, u32[]{:S(2)}) %copy-start) | copy-done | bytes 524312
  11.1 0.6 %shard_map.77 = (bf16[8,1,128,128]{3,2,1,0:T(8,128)(2,1)S(1)}, bf16[8,1,128,128]{3,2,1,0:T(8,128)(2,1)S(1)}, s32[8,1]{1,0:T(8,128)S(1)}, f32[8,128]{1,0:T(8,128)S(1)}) custom-call(f32[8,1,128,128]{3,2,1,0:T(8,128)S(1)} %copy-done, s32[8]{0:T(128)S(1)} %bitcast.10, s32[8,1]{1,0:T(8,128)S(1)} %copy.8.neighbours, f32[1,128]{1,0:T(1,128)S(1)} %copy-done.4, ...), custom_call_target="tpu_custom_call" | custom-call | flops 524288 | bytes 1048576 | tf_op jit(solution)/shard_map/pallas_call | solution.py:164
  11.7 5.3 %all-to-all-done.table = f32[32,8,128]{2,1,0:T(8,128)S(1)} async-done(((f32[32,8,128]{2,1,0:T(8,128)}), f32[32,8,128]{2,1,0:T(8,128)S(1)}, u32[]{:S(2)}, u32[]{:S(2)}) %all-to-all-start) | async-done | bytes 131104 | tf_op jit(solution)/shard_map/all_to_all | solution.py:176
  17.0 0.4 %shard_map.78 = f32[8,8,128]{2,1,0:T(8,128)S(1)} custom-call(f32[32,8,128]{2,1,0:T(8,128)S(1)} %all-to-all-done.table, bf16[8,1,128,128]{3,2,1,0:T(8,128)(2,1)S(1)} %get-tuple-element.12.high, bf16[8,1,128,128]{3,2,1,0:T(8,128)(2,1)S(1)} %get-tuple-element.13.low, s32[8,1]{1,0:T(8,128)S(1)} %get-tuple-element.14.sources, f32[8,128]{1,0:T(8,128)S(1)} %get-tuple-element.15.diagonal), custom_call_target="tpu_custom_call" | custom-call | flops 2097152 | bytes 524288 | tf_op jit(solution)/shard_map/pallas_call | solution.py:177
  17.4 1.2 %collective-permute-start = (f32[8,8,128]{2,1,0:T(8,128)S(1)}, f32[8,8,128]{2,1,0:T(8,128)S(1)}, u32[]{:S(2)}, u32[]{:S(2)}) collective-permute-start(f32[8,8,128]{2,1,0:T(8,128)S(1)} %shard_map.78), channel_id=1, source_target_pairs={{0,1},{1,0},{2,3},{3,2},{4,5},{5,4},{6,7},{7,6},{8,9},{9,8},{10,11... | collective-permute-start | bytes 98312 | tf_op jit(solution)/shard_map/ppermute | solution.py:15
  18.7 2.7 %collective-permute-done = f32[8,8,128]{2,1,0:T(8,128)S(1)} collective-permute-done((f32[8,8,128]{2,1,0:T(8,128)S(1)}, f32[8,8,128]{2,1,0:T(8,128)S(1)}, u32[]{:S(2)}, u32[]{:S(2)}) %collective-permute-start) | collective-permute-done | bytes 32800 | tf_op jit(solution)/shard_map/ppermute | solution.py:15
  21.4 1.0 %collective-permute-start.1 = (f32[8,8,128]{2,1,0:T(8,128)S(1)}, f32[8,8,128]{2,1,0:T(8,128)S(1)}, u32[]{:S(2)}, u32[]{:S(2)}) collective-permute-start(f32[8,8,128]{2,1,0:T(8,128)S(1)} %add.9), channel_id=1, source_target_pairs={{0,2},{1,3},{2,0},{3,1},{4,6},{5,7},{6,4},{7,5},{8,10},{9,11},{10,... | collective-permute-start | bytes 98312 | tf_op jit(solution)/shard_map/ppermute | solution.py:15
  22.4 2.9 %collective-permute-done.1 = f32[8,8,128]{2,1,0:T(8,128)S(1)} collective-permute-done((f32[8,8,128]{2,1,0:T(8,128)S(1)}, f32[8,8,128]{2,1,0:T(8,128)S(1)}, u32[]{:S(2)}, u32[]{:S(2)}) %collective-permute-start.1) | collective-permute-done | bytes 32800 | tf_op jit(solution)/shard_map/ppermute | solution.py:15
  25.3 1.4 %collective-permute-start.2 = (f32[8,8,128]{2,1,0:T(8,128)S(1)}, f32[8,8,128]{2,1,0:T(8,128)S(1)}, u32[]{:S(2)}, u32[]{:S(2)}) collective-permute-start(f32[8,8,128]{2,1,0:T(8,128)S(1)} %add.10.mine), channel_id=1, source_target_pairs={{0,4},{1,5},{2,6},{3,7},{4,0},{5,1},{6,2},{7,3},{8,12},{9,13},{10,... | collective-permute-start | bytes 98312 | tf_op jit(solution)/shard_map/ppermute | solution.py:15
  26.6 3.5 %collective-permute-done.2.theirs = f32[8,8,128]{2,1,0:T(8,128)S(1)} collective-permute-done((f32[8,8,128]{2,1,0:T(8,128)S(1)}, f32[8,8,128]{2,1,0:T(8,128)S(1)}, u32[]{:S(2)}, u32[]{:S(2)}) %collective-permute-start.2) | collective-permute-done | bytes 32800 | tf_op jit(solution)/shard_map/ppermute | solution.py:15
  30.1 0.2 shard_map.79
  30.3 1.3 %collective-permute-start.3 = (f32[8,128]{1,0:T(8,128)S(1)}, f32[8,128]{1,0:T(8,128)S(1)}, u32[]{:S(2)}, u32[]{:S(2)}) collective-permute-start(f32[8,128]{1,0:T(8,128)S(1)} %get-tuple-element.16), channel_id=1, source_target_pairs={{0,16},{8,24},{16,0},{24,8},{1,17},{9,25},{17,1},{25,9},{2,18},{10... | collective-permute-start | bytes 12296 | tf_op jit(solution)/shard_map/ppermute | solution.py:15
  31.6 2.3 %collective-permute-done.3 = f32[8,128]{1,0:T(8,128)S(1)} collective-permute-done((f32[8,128]{1,0:T(8,128)S(1)}, f32[8,128]{1,0:T(8,128)S(1)}, u32[]{:S(2)}, u32[]{:S(2)}) %collective-permute-start.3) | collective-permute-done | bytes 4128 | tf_op jit(solution)/shard_map/ppermute | solution.py:15
  33.9 0.0 collective-permute-start.4
  33.9 0.9 %shard_map.80.solved = f32[24,128]{1,0:T(8,128)S(1)} custom-call(f32[32,8,128]{2,1,0:T(8,128)S(1)} %all-to-all-done.table), custom_call_target="tpu_custom_call" | custom-call | flops 1000000 | bytes 131072 | tf_op jit(solution)/shard_map/pallas_call | solution.py:180
  34.9 0.2 collective-permute-done.4.theirs
  35.1 0.7 %shard_map.81 = (f32[1,8,128]{2,1,0:T(8,128)}, f32[1,8,128]{2,1,0:T(8,128)}, f32[8]{0:T(128)}) custom-call(f32[8,128]{1,0:T(8,128)S(1)} %add.11.mine, f32[8,128]{1,0:T(8,128)S(1)} %collective-permute-done.4.theirs, f32[24,128]{1,0:T(8,128)S(1)} %shard_map.80.solved, f32[8,128]{1,0:T(8,128)S(1)} %get-tuple-element.17.own), custom_call_target="tpu_custom_call" | custom-call | flops 10000 | bytes 100000 | tf_op jit(solution)/shard_map/pallas_call | solution.py:199
  (3 shorter events, 0.0 us)
Async XLA Ops:
  0.6 0.7 %copy-start.1 = (f32[8,1,128]{2,1,0:T(1,128)S(1)}, f32[8,1,128]{2,1,0:T(1,128)}, u32[]{:S(2)}) copy-start(f32[8,1,128]{2,1,0:T(1,128)} %param.5) | copy-start | bytes 12292
  2.0 7.3 %copy-start.5 = (s32[8,1]{0,1:T(1,128)S(1)}, s32[8,1]{0,1:T(1,128)}, u32[]{:S(2)}) copy-start(s32[8,1]{0,1:T(1,128)} %param.7) | copy-start | bytes 100
  2.0 15.0 %all-to-all-start = ((f32[32,8,128]{2,1,0:T(8,128)}), f32[32,8,128]{2,1,0:T(8,128)S(1)}, u32[]{:S(2)}, u32[]{:S(2)}) async-start(f32[32,8,128]{2,1,0:T(8,128)} %shard_map.76), calls=%async_computation | async-start | bytes 262144 | tf_op jit(solution)/shard_map/all_to_all | solution.py:176
  9.3 0.7 %copy-start.2 = (f32[8,1,128]{2,1,0:T(1,128)S(1)}, f32[8,1,128]{2,1,0:T(1,128)}, u32[]{:S(2)}) copy-start(f32[8,1,128]{2,1,0:T(1,128)} %param.5) | copy-start | bytes 12292
  9.4 0.7 %copy-start.3 = (s32[8,1]{0,1:T(1,128)S(1)}, s32[8,1]{0,1:T(1,128)}, u32[]{:S(2)}) copy-start(s32[8,1]{0,1:T(1,128)} %param.8) | copy-start | bytes 100
  9.4 0.7 %copy-start.4 = (f32[1,128]{1,0:T(1,128)S(1)}, f32[1,128]{1,0:T(1,128)}, u32[]{:S(2)}) copy-start(f32[1,128]{1,0:T(1,128)} %energies.1) | copy-start | bytes 1540
  10.1 1.0 %copy-start = (f32[8,1,128,128]{3,2,1,0:T(8,128)S(1)}, f32[8,1,128,128]{3,2,1,0:T(8,128)}, u32[]{:S(2)}) copy-start(f32[8,1,128,128]{3,2,1,0:T(8,128)} %couplings.1) | copy-start | bytes 1572868
  17.4 3.9 %collective-permute-start = (f32[8,8,128]{2,1,0:T(8,128)S(1)}, f32[8,8,128]{2,1,0:T(8,128)S(1)}, u32[]{:S(2)}, u32[]{:S(2)}) collective-permute-start(f32[8,8,128]{2,1,0:T(8,128)S(1)} %shard_map.78), channel_id=1, source_target_pairs={{0,1},{1,0},{2,3},{3,2},{4,5},{5,4},{6,7},{7,6},{8,9},{9,8},{10,11... | collective-permute-start | bytes 98312 | tf_op jit(solution)/shard_map/ppermute | solution.py:15
  21.4 3.9 %collective-permute-start.1 = (f32[8,8,128]{2,1,0:T(8,128)S(1)}, f32[8,8,128]{2,1,0:T(8,128)S(1)}, u32[]{:S(2)}, u32[]{:S(2)}) collective-permute-start(f32[8,8,128]{2,1,0:T(8,128)S(1)} %add.9), channel_id=1, source_target_pairs={{0,2},{1,3},{2,0},{3,1},{4,6},{5,7},{6,4},{7,5},{8,10},{9,11},{10,... | collective-permute-start | bytes 98312 | tf_op jit(solution)/shard_map/ppermute | solution.py:15
  25.3 4.8 %collective-permute-start.2 = (f32[8,8,128]{2,1,0:T(8,128)S(1)}, f32[8,8,128]{2,1,0:T(8,128)S(1)}, u32[]{:S(2)}, u32[]{:S(2)}) collective-permute-start(f32[8,8,128]{2,1,0:T(8,128)S(1)} %add.10.mine), channel_id=1, source_target_pairs={{0,4},{1,5},{2,6},{3,7},{4,0},{5,1},{6,2},{7,3},{8,12},{9,13},{10,... | collective-permute-start | bytes 98312 | tf_op jit(solution)/shard_map/ppermute | solution.py:15
  30.3 3.6 %collective-permute-start.3 = (f32[8,128]{1,0:T(8,128)S(1)}, f32[8,128]{1,0:T(8,128)S(1)}, u32[]{:S(2)}, u32[]{:S(2)}) collective-permute-start(f32[8,128]{1,0:T(8,128)S(1)} %get-tuple-element.16), channel_id=1, source_target_pairs={{0,16},{8,24},{16,0},{24,8},{1,17},{9,25},{17,1},{25,9},{2,18},{10... | collective-permute-start | bytes 12296 | tf_op jit(solution)/shard_map/ppermute | solution.py:15
  33.9 1.2 %collective-permute-start.4 = (f32[8,128]{1,0:T(8,128)S(1)}, f32[8,128]{1,0:T(8,128)S(1)}, u32[]{:S(2)}, u32[]{:S(2)}) collective-permute-start(f32[8,128]{1,0:T(8,128)S(1)} %add.11.mine), channel_id=1, source_target_pairs={{0,8},{8,0},{16,24},{24,16},{1,9},{9,1},{17,25},{25,17},{2,10},{10... | collective-permute-start | bytes 12296 | tf_op jit(solution)/shard_map/ppermute | solution.py:15

commit v3 on v2

--- a/solution.py
+++ b/solution.py
@@ -24,9 +24,15 @@
     return high, (x - high.astype(jnp.float32)).astype(jnp.bfloat16)
 
 
-def spread(row, copies):
-    for i in range(copies.shape[0]):
-        copies[i] = row[0]
+def spread(row, copies, own, filled, sem):
+    move = pltpu.make_async_copy(row, own, sem)
+    move.start()
+    move.wait()
+    for i in range(filled.shape[0]):
+        filled[i] = own[0]
+    move = pltpu.make_async_copy(filled, copies, sem)
+    move.start()
+    move.wait()
 
 
 def prepare(couplings, live, neighbours, energies, row, high, low, sources, diagonal):
@@ -113,9 +119,12 @@
     )
 
 
-def finish(mine, theirs, solved, own, sigma, residual, norms):
-    vectors, states = mine.shape
-    gram = mine[...] + theirs[...]
+def finish(*refs):
+    pieces, (solved, own, sigma, residual, norms) = refs[:-5], refs[-5:]
+    vectors, states = own.shape
+    gram = pieces[0][...]
+    for piece in pieces[1:]:
+        gram = gram + piece[...]
     lane = lax.broadcasted_iota(jnp.int32, (vectors, states), 1)
     sublane = lax.broadcasted_iota(jnp.int32, (vectors, states), 0)
     left = own[...]
@@ -158,8 +167,17 @@
 
     size = couplings.size
     row = jnp.transpose(trial_vectors, (1, 0, 2))
-    copies = call(
-        spread, shape(src_count * tgt_count, vectors, states), [VMEM], 0, 10**5
+    count = src_count * tgt_count
+    copies = pl.pallas_call(
+        spread,
+        out_shape=shape(count, vectors, states),
+        in_specs=[pl.BlockSpec(memory_space=pl.ANY)],
+        out_specs=pl.BlockSpec(memory_space=pl.ANY),
+        scratch_shapes=[
+            pltpu.VMEM(row.shape, jnp.float32),
+            pltpu.VMEM((count, vectors, states), jnp.float32),
+            pltpu.SemaphoreType.DMA(()),
+        ],
     )(row)
     high, low, sources, diagonal = call(
         prepare,
@@ -183,6 +201,7 @@
         theirs = exchange(partial, "src", bit)
         if 2 * bit < src_count:
             partial = partial + theirs
+            partial, solved = lax.optimization_barrier((partial, solved))
     own, gram = call(
         grams,
         (shape(vectors, states), shape(vectors, states)),
@@ -192,17 +211,16 @@
         [pltpu.VMEM((targets, vectors, states), jnp.float32)],
     )(partial, theirs, table)
 
-    for bit in reversed(bits_of(tgt_count)):
-        theirs = exchange(gram, "tgt", bit)
-        if bit > 1:
-            gram = gram + theirs
+    for bit in reversed(bits_of(tgt_count)[2:]):
+        gram = gram + exchange(gram, "tgt", bit)
+    pieces = [gram] + [exchange(gram, "tgt", bit) for bit in reversed(range(1, min(tgt_count, 4)))]
     sigma, residual, norms = call(
         finish,
         (shape(1, vectors, states), shape(1, vectors, states), shape(vectors)),
-        [VMEM] * 4,
+        [VMEM] * (len(pieces) + 2),
         10**4,
         10**5,
-    )(gram, theirs, solved, own)
+    )(*pieces, solved, own)
     return (jnp.transpose(sigma, (1, 0, 2)), jnp.transpose(residual, (1, 0, 2)), norms)
 
 

time: 36 us -> 34.9 us (0.969)
  waiting for transfers between devices: 16.8 us -> 15.2 us
  Pallas kernels: 3.48 us -> 4.18 us
  local copies, waits for them, and re-layouts: 2.48 us -> 1.8 us
  starting transfers between devices: 12.3 us -> 12.8 us
    ppermute x5 -> x6, waiting for transfers between devices: 11.5 us -> 9.88 us  [exchange(): return lax.ppermute(x, axis, [(i, i ^ bit) for i in range(count)])]
    pallas_call x1, Pallas kernels: 0.67 us -> 1.36 us  [shards(): pl.pallas_call(spread, out_shape=shape(count, vectors, states), in_specs=...]
    unnamed x13 -> x11, local copies, waits for them, and re-layouts: 2.48 us -> 1.8 us
    ppermute x5 -> x6, starting transfers between devices: 4.97 us -> 5.5 us  [exchange(): return lax.ppermute(x, axis, [(i, i ^ bit) for i in range(count)])]
  transfers between devices with their start and end apart: 6 -> 7, of which waited for: 6 -> 6; matrix products, arithmetic and copies ran while one was open for 0% -> 0% of each run, Pallas kernels for 4% -> 4%
where the time goes in v3:
time: 34.9 us; the launch traced here: 34.7 us
  waiting for transfers between devices  15.2 us (44%)
  starting transfers between devices  12.8 us (37%)
  Pallas kernels  4.18 us (12%)
  local copies, waits for them, and re-layouts  1.8 us (5%)
  between operations  0.69 us (2%)
    ppermute x6, waiting for transfers between devices, exchange(): return lax.ppermute(x, axis, [(i, i ^ bit) for i in range(count)])  9.88 us
    all_to_all x1, starting transfers between devices, shards(): table = lax.all_to_all(copies, ('tgt', 'src'), 0, 0, tiled=True)  7.3 us
    ppermute x6, starting transfers between devices, exchange(): return lax.ppermute(x, axis, [(i, i ^ bit) for i in range(count)])  5.5 us
    all_to_all x1, waiting for transfers between devices, shards(): table = lax.all_to_all(copies, ('tgt', 'src'), 0, 0, tiled=True)  5.3 us
    unnamed x11, local copies, waits for them, and re-layouts  1.8 us
    pallas_call x1, Pallas kernels, shards(): pl.pallas_call(spread, out_shape=shape(count, vectors, states), in_specs=...  1.36 us
    pallas_call x1, Pallas kernels, shards(): call(invert, shape(3 * vectors, states), [VMEM], 10 ** 6, 4 * table.size)  0.95 us
  transfers between devices with their start and end apart: 7, of which 6 were waited for; matrix products, arithmetic and copies ran while one was open for 0% of the time, Pallas kernels for 4%

profile of v3, /device:TPU:0, one launch (start us, length us, event | category | flops | bytes accessed | tf_op | source)
XLA Modules:
  0.0 34.7 jit_solution(16165381921933335888)
XLA Ops:
  0.6 1.4 %shard_map.76 = f32[32,8,128]{2,1,0:T(8,128)} custom-call(f32[1,8,128]{2,1,0:T(8,128)} %bitcast.8), custom_call_target="tpu_custom_call" | custom-call | tf_op jit(solution)/shard_map/pallas_call | solution.py:171
  2.0 0.0 copy-start.4
  2.0 7.3 %all-to-all-start = ((f32[32,8,128]{2,1,0:T(8,128)}), f32[32,8,128]{2,1,0:T(8,128)S(1)}, u32[]{:S(2)}, u32[]{:S(2)}) async-start(f32[32,8,128]{2,1,0:T(8,128)} %shard_map.76), calls=%async_computation | async-start | bytes 262144 | tf_op jit(solution)/shard_map/all_to_all | solution.py:194
  9.3 0.0 copy-done.4
  9.3 0.0 copy-start.1
  9.3 0.1 copy.8.neighbours
  9.4 0.0 copy-start.2
  9.4 0.0 copy-start.3
  9.4 0.6 %copy-done.1 = f32[8,1,128]{2,1,0:T(1,128)S(1)} copy-done((f32[8,1,128]{2,1,0:T(1,128)S(1)}, f32[8,1,128]{2,1,0:T(1,128)}, u32[]{:S(2)}) %copy-start.1) | copy-done | bytes 4120
  10.0 0.1 copy-done.2
  10.1 0.0 copy-done.3
  10.1 0.0 copy-start
  10.1 1.0 %copy-done = f32[8,1,128,128]{3,2,1,0:T(8,128)S(1)} copy-done((f32[8,1,128,128]{3,2,1,0:T(8,128)S(1)}, f32[8,1,128,128]{3,2,1,0:T(8,128)}, u32[]{:S(2)}) %copy-start) | copy-done | bytes 524312
  11.1 0.6 %shard_map.77 = (bf16[8,1,128,128]{3,2,1,0:T(8,128)(2,1)S(1)}, bf16[8,1,128,128]{3,2,1,0:T(8,128)(2,1)S(1)}, s32[8,1]{1,0:T(8,128)S(1)}, f32[8,128]{1,0:T(8,128)S(1)}) custom-call(f32[8,1,128,128]{3,2,1,0:T(8,128)S(1)} %copy-done, s32[8]{0:T(128)S(1)} %bitcast.10, s32[8,1]{1,0:T(8,128)S(1)} %copy.8.neighbours, f32[1,128]{1,0:T(1,128)S(1)} %copy-done.3, ...), custom_call_target="tpu_custom_call" | custom-call | flops 524288 | bytes 1048576 | tf_op jit(solution)/shard_map/pallas_call | solution.py:182
  11.8 5.3 %all-to-all-done.table = f32[32,8,128]{2,1,0:T(8,128)S(1)} async-done(((f32[32,8,128]{2,1,0:T(8,128)}), f32[32,8,128]{2,1,0:T(8,128)S(1)}, u32[]{:S(2)}, u32[]{:S(2)}) %all-to-all-start) | async-done | bytes 131104 | tf_op jit(solution)/shard_map/all_to_all | solution.py:194
  17.1 0.4 %shard_map.78 = f32[8,8,128]{2,1,0:T(8,128)S(1)} custom-call(f32[32,8,128]{2,1,0:T(8,128)S(1)} %all-to-all-done.table, bf16[8,1,128,128]{3,2,1,0:T(8,128)(2,1)S(1)} %get-tuple-element.16.high, bf16[8,1,128,128]{3,2,1,0:T(8,128)(2,1)S(1)} %get-tuple-element.17.low, s32[8,1]{1,0:T(8,128)S(1)} %get-tuple-element.18.sources, f32[8,128]{1,0:T(8,128)S(1)} %get-tuple-element.19.diagonal), custom_call_target="tpu_custom_call" | custom-call | flops 2097152 | bytes 524288 | tf_op jit(solution)/shard_map/pallas_call | solution.py:195
  17.4 1.2 %collective-permute-start = (f32[8,8,128]{2,1,0:T(8,128)S(1)}, f32[8,8,128]{2,1,0:T(8,128)S(1)}, u32[]{:S(2)}, u32[]{:S(2)}) collective-permute-start(f32[8,8,128]{2,1,0:T(8,128)S(1)} %shard_map.78), channel_id=1, source_target_pairs={{0,1},{1,0},{2,3},{3,2},{4,5},{5,4},{6,7},{7,6},{8,9},{9,8},{10,11... | collective-permute-start | bytes 98312 | tf_op jit(solution)/shard_map/ppermute | solution.py:15
  18.7 0.9 %shard_map.79.refs_4_ = f32[24,128]{1,0:T(8,128)S(1)} custom-call(f32[32,8,128]{2,1,0:T(8,128)S(1)} %all-to-all-done.table), custom_call_target="tpu_custom_call" | custom-call | flops 1000000 | bytes 131072 | tf_op jit(solution)/shard_map/pallas_call | solution.py:198
  19.6 1.7 %collective-permute-done = f32[8,8,128]{2,1,0:T(8,128)S(1)} collective-permute-done((f32[8,8,128]{2,1,0:T(8,128)S(1)}, f32[8,8,128]{2,1,0:T(8,128)S(1)}, u32[]{:S(2)}, u32[]{:S(2)}) %collective-permute-start) | collective-permute-done | bytes 32800 | tf_op jit(solution)/shard_map/ppermute | solution.py:15
  21.4 1.0 %collective-permute-start.1 = (f32[8,8,128]{2,1,0:T(8,128)S(1)}, f32[8,8,128]{2,1,0:T(8,128)S(1)}, u32[]{:S(2)}, u32[]{:S(2)}) collective-permute-start(f32[8,8,128]{2,1,0:T(8,128)S(1)} %add.6), channel_id=1, source_target_pairs={{0,2},{1,3},{2,0},{3,1},{4,6},{5,7},{6,4},{7,5},{8,10},{9,11},{10,... | collective-permute-start | bytes 98312 | tf_op jit(solution)/shard_map/ppermute | solution.py:15
  22.4 2.9 %collective-permute-done.1 = f32[8,8,128]{2,1,0:T(8,128)S(1)} collective-permute-done((f32[8,8,128]{2,1,0:T(8,128)S(1)}, f32[8,8,128]{2,1,0:T(8,128)S(1)}, u32[]{:S(2)}, u32[]{:S(2)}) %collective-permute-start.1) | collective-permute-done | bytes 32800 | tf_op jit(solution)/shard_map/ppermute | solution.py:15
  25.3 1.4 %collective-permute-start.2 = (f32[8,8,128]{2,1,0:T(8,128)S(1)}, f32[8,8,128]{2,1,0:T(8,128)S(1)}, u32[]{:S(2)}, u32[]{:S(2)}) collective-permute-start(f32[8,8,128]{2,1,0:T(8,128)S(1)} %add.7.mine), channel_id=1, source_target_pairs={{0,4},{1,5},{2,6},{3,7},{4,0},{5,1},{6,2},{7,3},{8,12},{9,13},{10,... | collective-permute-start | bytes 98312 | tf_op jit(solution)/shard_map/ppermute | solution.py:15
  26.7 3.5 %collective-permute-done.2.theirs = f32[8,8,128]{2,1,0:T(8,128)S(1)} collective-permute-done((f32[8,8,128]{2,1,0:T(8,128)S(1)}, f32[8,8,128]{2,1,0:T(8,128)S(1)}, u32[]{:S(2)}, u32[]{:S(2)}) %collective-permute-start.2) | collective-permute-done | bytes 32800 | tf_op jit(solution)/shard_map/ppermute | solution.py:15
  30.1 0.2 shard_map.80
  30.3 0.0 collective-permute-start.3
  30.3 1.4 %collective-permute-start.4 = (f32[8,128]{1,0:T(8,128)S(1)}, f32[8,128]{1,0:T(8,128)S(1)}, u32[]{:S(2)}, u32[]{:S(2)}) collective-permute-start(f32[8,128]{1,0:T(8,128)S(1)} %get-tuple-element.23.refs_0_), channel_id=1, source_target_pairs={{0,16},{8,24},{16,0},{24,8},{1,17},{9,25},{17,1},{25,9},{2,18},{10... | collective-permute-start | bytes 12296 | tf_op jit(solution)/shard_map/ppermute | solution.py:15
  31.7 0.5 %collective-permute-start.5 = (f32[8,128]{1,0:T(8,128)S(1)}, f32[8,128]{1,0:T(8,128)S(1)}, u32[]{:S(2)}, u32[]{:S(2)}) collective-permute-start(f32[8,128]{1,0:T(8,128)S(1)} %get-tuple-element.23.refs_0_), channel_id=1, source_target_pairs={{0,8},{8,0},{16,24},{24,16},{1,9},{9,1},{17,25},{25,17},{2,10},{10... | collective-permute-start | bytes 12296 | tf_op jit(solution)/shard_map/ppermute | solution.py:15
  32.2 1.2 %collective-permute-done.3.refs_1_ = f32[8,128]{1,0:T(8,128)S(1)} collective-permute-done((f32[8,128]{1,0:T(8,128)S(1)}, f32[8,128]{1,0:T(8,128)S(1)}, u32[]{:S(2)}, u32[]{:S(2)}) %collective-permute-start.3) | collective-permute-done | bytes 4128 | tf_op jit(solution)/shard_map/ppermute | solution.py:15
  33.4 0.6 %collective-permute-done.4.refs_2_ = f32[8,128]{1,0:T(8,128)S(1)} collective-permute-done((f32[8,128]{1,0:T(8,128)S(1)}, f32[8,128]{1,0:T(8,128)S(1)}, u32[]{:S(2)}, u32[]{:S(2)}) %collective-permute-start.4) | collective-permute-done | bytes 4128 | tf_op jit(solution)/shard_map/ppermute | solution.py:15
  34.0 0.0 collective-permute-done.5.refs_3_
  34.0 0.7 %shard_map.81 = (f32[1,8,128]{2,1,0:T(8,128)}, f32[1,8,128]{2,1,0:T(8,128)}, f32[8]{0:T(128)}) custom-call(f32[8,128]{1,0:T(8,128)S(1)} %get-tuple-element.23.refs_0_, f32[8,128]{1,0:T(8,128)S(1)} %collective-permute-done.3.refs_1_, f32[8,128]{1,0:T(8,128)S(1)} %collective-permute-done.4.refs_2_, f32[8,128]{1,0:T(8,128)S(1)} %collective-permute-done.5.refs_3_, ...), custom_call_target="tpu_custom_call" | custom-call | flops 10000 | bytes 100000 | tf_op jit(solution)/shard_map/pallas_call | solution.py:217
  (2 shorter events, 0.0 us)
Async XLA Ops:
  2.0 7.3 %copy-start.4 = (s32[8,1]{0,1:T(1,128)S(1)}, s32[8,1]{0,1:T(1,128)}, u32[]{:S(2)}) copy-start(s32[8,1]{0,1:T(1,128)} %param.7) | copy-start | bytes 100
  2.0 15.1 %all-to-all-start = ((f32[32,8,128]{2,1,0:T(8,128)}), f32[32,8,128]{2,1,0:T(8,128)S(1)}, u32[]{:S(2)}, u32[]{:S(2)}) async-start(f32[32,8,128]{2,1,0:T(8,128)} %shard_map.76), calls=%async_computation | async-start | bytes 262144 | tf_op jit(solution)/shard_map/all_to_all | solution.py:194
  9.3 0.7 %copy-start.1 = (f32[8,1,128]{2,1,0:T(1,128)S(1)}, f32[8,1,128]{2,1,0:T(1,128)}, u32[]{:S(2)}) copy-start(f32[8,1,128]{2,1,0:T(1,128)} %param.5) | copy-start | bytes 12292
  9.4 0.7 %copy-start.2 = (s32[8,1]{0,1:T(1,128)S(1)}, s32[8,1]{0,1:T(1,128)}, u32[]{:S(2)}) copy-start(s32[8,1]{0,1:T(1,128)} %param.8) | copy-start | bytes 100
  9.4 0.7 %copy-start.3 = (f32[1,128]{1,0:T(1,128)S(1)}, f32[1,128]{1,0:T(1,128)}, u32[]{:S(2)}) copy-start(f32[1,128]{1,0:T(1,128)} %energies.1) | copy-start | bytes 1540
  10.1 1.0 %copy-start = (f32[8,1,128,128]{3,2,1,0:T(8,128)S(1)}, f32[8,1,128,128]{3,2,1,0:T(8,128)}, u32[]{:S(2)}) copy-start(f32[8,1,128,128]{3,2,1,0:T(8,128)} %couplings.1) | copy-start | bytes 1572868
  17.4 3.9 %collective-permute-start = (f32[8,8,128]{2,1,0:T(8,128)S(1)}, f32[8,8,128]{2,1,0:T(8,128)S(1)}, u32[]{:S(2)}, u32[]{:S(2)}) collective-permute-start(f32[8,8,128]{2,1,0:T(8,128)S(1)} %shard_map.78), channel_id=1, source_target_pairs={{0,1},{1,0},{2,3},{3,2},{4,5},{5,4},{6,7},{7,6},{8,9},{9,8},{10,11... | collective-permute-start | bytes 98312 | tf_op jit(solution)/shard_map/ppermute | solution.py:15
  21.4 3.9 %collective-permute-start.1 = (f32[8,8,128]{2,1,0:T(8,128)S(1)}, f32[8,8,128]{2,1,0:T(8,128)S(1)}, u32[]{:S(2)}, u32[]{:S(2)}) collective-permute-start(f32[8,8,128]{2,1,0:T(8,128)S(1)} %add.6), channel_id=1, source_target_pairs={{0,2},{1,3},{2,0},{3,1},{4,6},{5,7},{6,4},{7,5},{8,10},{9,11},{10,... | collective-permute-start | bytes 98312 | tf_op jit(solution)/shard_map/ppermute | solution.py:15
  25.3 4.8 %collective-permute-start.2 = (f32[8,8,128]{2,1,0:T(8,128)S(1)}, f32[8,8,128]{2,1,0:T(8,128)S(1)}, u32[]{:S(2)}, u32[]{:S(2)}) collective-permute-start(f32[8,8,128]{2,1,0:T(8,128)S(1)} %add.7.mine), channel_id=1, source_target_pairs={{0,4},{1,5},{2,6},{3,7},{4,0},{5,1},{6,2},{7,3},{8,12},{9,13},{10,... | collective-permute-start | bytes 98312 | tf_op jit(solution)/shard_map/ppermute | solution.py:15
  30.3 3.0 %collective-permute-start.3 = (f32[8,128]{1,0:T(8,128)S(1)}, f32[8,128]{1,0:T(8,128)S(1)}, u32[]{:S(2)}, u32[]{:S(2)}) collective-permute-start(f32[8,128]{1,0:T(8,128)S(1)} %get-tuple-element.23.refs_0_), channel_id=1, source_target_pairs={{0,24},{8,16},{16,8},{24,0},{1,25},{9,17},{17,9},{25,1},{2,26},{10... | collective-permute-start | bytes 12296 | tf_op jit(solution)/shard_map/ppermute | solution.py:15
  30.3 3.7 %collective-permute-start.4 = (f32[8,128]{1,0:T(8,128)S(1)}, f32[8,128]{1,0:T(8,128)S(1)}, u32[]{:S(2)}, u32[]{:S(2)}) collective-permute-start(f32[8,128]{1,0:T(8,128)S(1)} %get-tuple-element.23.refs_0_), channel_id=1, source_target_pairs={{0,16},{8,24},{16,0},{24,8},{1,17},{9,25},{17,1},{25,9},{2,18},{10... | collective-permute-start | bytes 12296 | tf_op jit(solution)/shard_map/ppermute | solution.py:15
  31.7 2.3 %collective-permute-start.5 = (f32[8,128]{1,0:T(8,128)S(1)}, f32[8,128]{1,0:T(8,128)S(1)}, u32[]{:S(2)}, u32[]{:S(2)}) collective-permute-start(f32[8,128]{1,0:T(8,128)S(1)} %get-tuple-element.23.refs_0_), channel_id=1, source_target_pairs={{0,8},{8,0},{16,24},{24,16},{1,9},{9,1},{17,25},{25,17},{2,10},{10... | collective-permute-start | bytes 12296 | tf_op jit(solution)/shard_map/ppermute | solution.py:15

commit v4 on v3

--- a/solution.py
+++ b/solution.py
@@ -6,7 +6,6 @@
 from jax.sharding import PartitionSpec as P
 
 VMEM = pl.BlockSpec(memory_space=pltpu.VMEM)
-SMEM = pl.BlockSpec(memory_space=pltpu.SMEM)
 LIMIT = 24 * 2**20
 
 
@@ -15,6 +14,16 @@
     return lax.ppermute(x, axis, [(i, i ^ bit) for i in range(count)])
 
 
+def pair(x, bits):
+    tgt_count, src_count = lax.axis_size("tgt"), lax.axis_size("src")
+    partners = [
+        (t * src_count + s, t * src_count + (s ^ bits[t % 2]))
+        for t in range(tgt_count)
+        for s in range(src_count)
+    ]
+    return lax.ppermute(x, ("tgt", "src"), partners)
+
+
 def bits_of(count):
     return [1 << n for n in range(count.bit_length() - 1)]
 
@@ -24,25 +33,41 @@
     return high, (x - high.astype(jnp.float32)).astype(jnp.bfloat16)
 
 
-def spread(row, copies, own, filled, sem):
-    move = pltpu.make_async_copy(row, own, sem)
-    move.start()
-    move.wait()
+def spread(row, neighbours, live, energies, copies, side, own, at, alive, energy, filled, packed, sems):
+    slots, targets = live.shape
+    vectors = own.shape[1]
+    inward = [
+        pltpu.make_async_copy(source, target, sems.at[n])
+        for n, (source, target) in enumerate(
+            [(row, own), (neighbours, at), (live, alive), (energies, energy)]
+        )
+    ]
+    for move in inward:
+        move.start()
+    inward[0].wait()
     for i in range(filled.shape[0]):
         filled[i] = own[0]
-    move = pltpu.make_async_copy(filled, copies, sem)
-    move.start()
-    move.wait()
-
-
-def prepare(couplings, live, neighbours, energies, row, high, low, sources, diagonal):
-    targets, slots = couplings.shape[0], couplings.shape[1]
+    outward = pltpu.make_async_copy(filled, copies, sems.at[0])
+    outward.start()
+    for move in inward[1:]:
+        move.wait()
+    packed[...] = jnp.zeros_like(packed)
+    packed[0:vectors] = own[0] * energy[...]
+    packed[vectors : vectors + slots, 0:targets] = at[...].astype(jnp.float32)
+    packed[vectors + slots : vectors + 2 * slots, 0:targets] = alive[...].astype(jnp.float32)
+    sent = pltpu.make_async_copy(packed, side, sems.at[1])
+    sent.start()
+    outward.wait()
+    sent.wait()
+
+
+def prepare(couplings, side, halves):
+    targets, slots, states = couplings.shape[:3]
+    first = side.shape[0] - slots
     for i in range(targets):
         for n in range(slots):
-            weight = live[i * slots + n].astype(jnp.float32)
-            high[i, n], low[i, n] = split(couplings[i, n] * weight)
-    sources[...] = neighbours[...]
-    diagonal[...] = row[0] * energies[...]
+            weight = side[first + n : first + n + 1, i : i + 1]
+            halves[i, n, :states], halves[i, n, states:] = split(couplings[i, n] * weight)
 
 
 def times(left, right):
@@ -51,19 +76,26 @@
     )
 
 
-def products(table, high, low, sources, diagonal, partial):
-    targets, slots = high.shape[0], high.shape[1]
-    vectors = table.shape[1]
+def products(table, halves, side, other_halves, other_side, partial):
+    targets, slots = halves.shape[0], halves.shape[1]
+    vectors, states = table.shape[1:]
     own_src = lax.axis_index("src")
-    at = sources[...]
+    away = 1 + lax.axis_index("tgt") % 2
+    at = side[vectors : vectors + slots].astype(jnp.int32)
+    other_at = other_side[vectors : vectors + slots].astype(jnp.int32)
     for i in range(targets):
         total = None
         for n in range(slots):
-            row = jnp.concatenate(split(table[at[i, n]]), axis=0)
-            term = times(row, high[i, n]) + times(row, low[i, n])
+            rows = jnp.concatenate([table[at[n, i]], table[other_at[n, i]]], axis=1)
+            term = times(
+                jnp.concatenate(split(rows), axis=0),
+                jnp.concatenate([halves[i, n], other_halves[i, n]], axis=1),
+            )
             total = term if total is None else total + term
+        total = total[:, :states] + total[:, states:]
         partial[i] = total[:vectors] + total[vectors:]
-    partial[own_src] = partial[own_src] + diagonal[...]
+    partial[own_src] = partial[own_src] + side[0:vectors]
+    partial[own_src ^ away] = partial[own_src ^ away] + other_side[0:vectors]
 
 
 def contract(left, right):
@@ -122,9 +154,10 @@
 def finish(*refs):
     pieces, (solved, own, sigma, residual, norms) = refs[:-5], refs[-5:]
     vectors, states = own.shape
-    gram = pieces[0][...]
-    for piece in pieces[1:]:
-        gram = gram + piece[...]
+    pieces = [piece[...] for piece in pieces]
+    while len(pieces) > 1:
+        pieces = [left + right for left, right in zip(pieces[::2], pieces[1::2])]
+    gram = pieces[0]
     lane = lax.broadcasted_iota(jnp.int32, (vectors, states), 1)
     sublane = lax.broadcasted_iota(jnp.int32, (vectors, states), 0)
     left = own[...]
@@ -167,39 +200,39 @@
 
     size = couplings.size
     row = jnp.transpose(trial_vectors, (1, 0, 2))
-    count = src_count * tgt_count
-    copies = pl.pallas_call(
+    count, slots = src_count * tgt_count, couplings.shape[1]
+    side_shape = (vectors + 2 * slots, states)
+    anywhere = pl.BlockSpec(memory_space=pl.ANY)
+    copies, side = pl.pallas_call(
         spread,
-        out_shape=shape(count, vectors, states),
-        in_specs=[pl.BlockSpec(memory_space=pl.ANY)],
-        out_specs=pl.BlockSpec(memory_space=pl.ANY),
+        out_shape=(shape(count, vectors, states), shape(*side_shape)),
+        in_specs=[anywhere] * 4,
+        out_specs=[anywhere] * 2,
         scratch_shapes=[
             pltpu.VMEM(row.shape, jnp.float32),
+            pltpu.VMEM((slots, targets), jnp.int32),
+            pltpu.VMEM((slots, targets), jnp.int32),
+            pltpu.VMEM(energies.shape, jnp.float32),
             pltpu.VMEM((count, vectors, states), jnp.float32),
-            pltpu.SemaphoreType.DMA(()),
+            pltpu.VMEM(side_shape, jnp.float32),
+            pltpu.SemaphoreType.DMA((4,)),
         ],
-    )(row)
-    high, low, sources, diagonal = call(
-        prepare,
-        (
-            shape(*couplings.shape, dtype=jnp.bfloat16),
-            shape(*couplings.shape, dtype=jnp.bfloat16),
-            shape(*neighbours.shape, dtype=jnp.int32),
-            shape(vectors, states),
-        ),
-        [VMEM, SMEM, VMEM, VMEM, VMEM],
-        4 * size,
-        8 * size,
-    )(couplings, live_slots.reshape(-1), neighbours, energies, row)
+    )(row, neighbours.T, live_slots.T, energies)
+    other_side = pair(side, (1, 2))
+    other = pair(couplings, (1, 2))
+    half = shape(targets, slots, 2 * states, states, dtype=jnp.bfloat16)
+    halve = call(prepare, half, [VMEM] * 2, 4 * size, 8 * size)
+    halves, other_halves = halve(couplings, side), halve(other, other_side)
     table = lax.all_to_all(copies, ("tgt", "src"), 0, 0, tiled=True)
     partial = call(
-        products, shape(targets, vectors, states), [VMEM] * 5, 2 * size * vectors, 4 * size
-    )(table, high, low, sources, diagonal)
+        products, shape(targets, vectors, states), [VMEM] * 5, 4 * size * vectors, 8 * size
+    )(table, halves, side, other_halves, other_side)
     solved = call(invert, shape(3 * vectors, states), [VMEM], 10**6, 4 * table.size)(table)
 
-    for bit in bits_of(src_count):
-        theirs = exchange(partial, "src", bit)
-        if 2 * bit < src_count:
+    steps = [(2, 1)] + [(bit, bit) for bit in bits_of(src_count)[2:]]
+    for n, step in enumerate(steps):
+        theirs = pair(partial, step)
+        if n + 1 < len(steps):
             partial = partial + theirs
             partial, solved = lax.optimization_barrier((partial, solved))
     own, gram = call(
@@ -213,7 +246,8 @@
 
     for bit in reversed(bits_of(tgt_count)[2:]):
         gram = gram + exchange(gram, "tgt", bit)
-    pieces = [gram] + [exchange(gram, "tgt", bit) for bit in reversed(range(1, min(tgt_count, 4)))]
+    pieces = [exchange(gram, "tgt", bit) for bit in reversed(range(1, min(tgt_count, 4)))]
+    pieces = pieces + [gram]
     sigma, residual, norms = call(
         finish,
         (shape(1, vectors, states), shape(1, vectors, states), shape(vectors)),

time: 34.9 us -> 31.7 us (0.908)
  waiting for transfers between devices: 15.2 us -> 11.6 us
  starting transfers between devices: 12.8 us -> 14.2 us
  local copies, waits for them, and re-layouts: 1.8 us -> 1.05 us
    ppermute x6 -> x3, waiting for transfers between devices: 9.88 us -> 1.79 us  [exchange(): return lax.ppermute(x, axis, [(i, i ^ bit) for i in range(count)])]
    ppermute x0 -> x4, starting transfers between devices: none -> 7.36 us  [pair(): return lax.ppermute(x, ('tgt', 'src'), partners)]
    ppermute x0 -> x4, waiting for transfers between devices: none -> 5.99 us  [pair(): return lax.ppermute(x, ('tgt', 'src'), partners)]
    ppermute x6 -> x3, starting transfers between devices: 5.5 us -> 1.88 us  [exchange(): return lax.ppermute(x, axis, [(i, i ^ bit) for i in range(count)])]
    all_to_all x1, starting transfers between devices: 7.3 us -> 4.93 us  [shards(): table = lax.all_to_all(copies, ('tgt', 'src'), 0, 0, tiled=True)]
    all_to_all x1, waiting for transfers between devices: 5.3 us -> 3.83 us  [shards(): table = lax.all_to_all(copies, ('tgt', 'src'), 0, 0, tiled=True)]
    unnamed x11 -> x4, local copies, waits for them, and re-layouts: 1.8 us -> 1.05 us
    pallas_call x3 -> x4, Pallas kernels: 2.36 us -> 2.14 us  [the longest x1 1.38 us: shards(): pl.pallas_call(spread, out_shape=(shape(count, vectors, states), shape(*s...]
  transfers between devices with their start and end apart: 7 -> 8, of which waited for: 6 -> 6; matrix products, arithmetic and copies ran while one was open for 0% -> 0% of each run, Pallas kernels for 4% -> 8%
where the time goes in v4:
time: 31.7 us; the launch traced here: 31.5 us
  starting transfers between devices  14.2 us (45%)
  waiting for transfers between devices  11.6 us (37%)
  Pallas kernels  3.96 us (12%)
  local copies, waits for them, and re-layouts  1.05 us (3%)
  between operations  0.69 us (2%)
    ppermute x4, starting transfers between devices, pair(): return lax.ppermute(x, ('tgt', 'src'), partners)  7.36 us
    ppermute x4, waiting for transfers between devices, pair(): return lax.ppermute(x, ('tgt', 'src'), partners)  5.99 us
    all_to_all x1, starting transfers between devices, shards(): table = lax.all_to_all(copies, ('tgt', 'src'), 0, 0, tiled=True)  4.93 us
    all_to_all x1, waiting for transfers between devices, shards(): table = lax.all_to_all(copies, ('tgt', 'src'), 0, 0, tiled=True)  3.83 us
    ppermute x3, starting transfers between devices, exchange(): return lax.ppermute(x, axis, [(i, i ^ bit) for i in range(count)])  1.88 us
    ppermute x3, waiting for transfers between devices, exchange(): return lax.ppermute(x, axis, [(i, i ^ bit) for i in range(count)])  1.79 us
    pallas_call x1, Pallas kernels, shards(): pl.pallas_call(spread, out_shape=(shape(count, vectors, states), shape(*s...  1.38 us
    unnamed x4, local copies, waits for them, and re-layouts  1.05 us
  transfers between devices with their start and end apart: 8, of which 6 were waited for; matrix products, arithmetic and copies ran while one was open for 0% of the time, Pallas kernels for 8%

profile of v4, /device:TPU:0, one launch (start us, length us, event | category | flops | bytes accessed | tf_op | source)
XLA Modules:
  0.0 31.5 jit_solution(11833762847388729481)
XLA Ops:
  0.6 3.0 %collective-permute-start = (f32[8,1,128,128]{3,2,1,0:T(8,128)}, f32[8,1,128,128]{3,2,1,0:T(8,128)S(1)}, u32[]{:S(2)}, u32[]{:S(2)}) collective-permute-start(f32[8,1,128,128]{3,2,1,0:T(8,128)} %couplings.1), channel_id=1, source_target_pairs={{0,1},{1,0},{2,3},{3,2},{4,5},{5,4},{6,7},{7,6},{8,10},{9,11},{10,... | collective-permute-start | bytes 1572872 | tf_op jit(solution)/shard_map/ppermute | solution.py:24
  3.6 1.4 %shard_map.76 = (f32[32,8,128]{2,1,0:T(8,128)}, f32[10,128]{1,0:T(8,128)}) custom-call(f32[1,8,128]{2,1,0:T(8,128)} %bitcast.9, s32[1,8]{1,0:T(1,128)} %bitcast.10, s32[1,8]{1,0:T(1,128)} %bitcast.11, f32[1,128]{1,0:T(1,128)} %energies.1), custom_call_target="tpu_custom_call" | custom-call | tf_op jit(solution)/shard_map/pallas_call | solution.py:206
  5.0 0.0 copy-start.1
  5.0 4.9 %all-to-all-start = ((f32[32,8,128]{2,1,0:T(8,128)}), f32[32,8,128]{2,1,0:T(8,128)S(1)}, u32[]{:S(2)}, u32[]{:S(2)}) async-start(f32[32,8,128]{2,1,0:T(8,128)} %get-tuple-element.12), calls=%async_computation | async-start | bytes 262144 | tf_op jit(solution)/shard_map/all_to_all | solution.py:226
  10.0 0.0 copy-done.1
  10.0 1.8 %collective-permute-start.1 = (f32[10,128]{1,0:T(8,128)S(1)}, f32[10,128]{1,0:T(8,128)S(1)}, u32[]{:S(2)}, u32[]{:S(2)}) collective-permute-start(f32[10,128]{1,0:T(8,128)S(1)} %copy-done.1), channel_id=1, source_target_pairs={{0,1},{1,0},{2,3},{3,2},{4,5},{5,4},{6,7},{7,6},{8,10},{9,11},{10,... | collective-permute-start | bytes 15368 | tf_op jit(solution)/shard_map/ppermute | solution.py:24
  11.8 0.0 copy-start
  11.8 1.0 %copy-done = f32[8,1,128,128]{3,2,1,0:T(8,128)S(1)} copy-done((f32[8,1,128,128]{3,2,1,0:T(8,128)S(1)}, f32[8,1,128,128]{3,2,1,0:T(8,128)}, u32[]{:S(2)}) %copy-start) | copy-done | bytes 524312
  12.9 0.2 shard_map.77.halves
  13.0 0.7 %collective-permute-done.1.side.other_side = f32[10,128]{1,0:T(8,128)S(1)} collective-permute-done((f32[10,128]{1,0:T(8,128)S(1)}, f32[10,128]{1,0:T(8,128)S(1)}, u32[]{:S(2)}, u32[]{:S(2)}) %collective-permute-start.1) | collective-permute-done | bytes 5152 | tf_op jit(solution)/shard_map/ppermute | solution.py:24
  13.7 0.0 collective-permute-done.couplings
  13.7 0.2 shard_map.78.other_halves
  13.9 3.8 %all-to-all-done.table = f32[32,8,128]{2,1,0:T(8,128)S(1)} async-done(((f32[32,8,128]{2,1,0:T(8,128)}), f32[32,8,128]{2,1,0:T(8,128)S(1)}, u32[]{:S(2)}, u32[]{:S(2)}) %all-to-all-start) | async-done | bytes 131104 | tf_op jit(solution)/shard_map/all_to_all | solution.py:226
  17.7 0.4 %shard_map.79 = f32[8,8,128]{2,1,0:T(8,128)S(1)} custom-call(f32[32,8,128]{2,1,0:T(8,128)S(1)} %all-to-all-done.table, bf16[8,1,256,128]{3,2,1,0:T(8,128)(2,1)S(1)} %shard_map.77.halves, f32[10,128]{1,0:T(8,128)S(1)} %copy-done.1, bf16[8,1,256,128]{3,2,1,0:T(8,128)(2,1)S(1)} %shard_map.78.other_halves, f32[10,128]{1,0:T(8,128)S(1)} %collective-permute-done.1.side.other_side), custom_call_target="tpu_custom_call" | custom-call | flops 4194304 | bytes 1048576 | tf_op jit(solution)/shard_map/pallas_call | solution.py:227
  18.1 1.1 %collective-permute-start.2 = (f32[8,8,128]{2,1,0:T(8,128)S(1)}, f32[8,8,128]{2,1,0:T(8,128)S(1)}, u32[]{:S(2)}, u32[]{:S(2)}) collective-permute-start(f32[8,8,128]{2,1,0:T(8,128)S(1)} %shard_map.79), channel_id=1, source_target_pairs={{0,2},{1,3},{2,0},{3,1},{4,6},{5,7},{6,4},{7,5},{8,9},{9,8},{10,11... | collective-permute-start | bytes 98312 | tf_op jit(solution)/shard_map/ppermute | solution.py:24
  19.2 0.9 %shard_map.80.refs_4_ = f32[24,128]{1,0:T(8,128)S(1)} custom-call(f32[32,8,128]{2,1,0:T(8,128)S(1)} %all-to-all-done.table), custom_call_target="tpu_custom_call" | custom-call | flops 1000000 | bytes 131072 | tf_op jit(solution)/shard_map/pallas_call | solution.py:230
  20.2 2.0 %collective-permute-done.2 = f32[8,8,128]{2,1,0:T(8,128)S(1)} collective-permute-done((f32[8,8,128]{2,1,0:T(8,128)S(1)}, f32[8,8,128]{2,1,0:T(8,128)S(1)}, u32[]{:S(2)}, u32[]{:S(2)}) %collective-permute-start.2) | collective-permute-done | bytes 32800 | tf_op jit(solution)/shard_map/ppermute | solution.py:24
  22.1 1.4 %collective-permute-start.3 = (f32[8,8,128]{2,1,0:T(8,128)S(1)}, f32[8,8,128]{2,1,0:T(8,128)S(1)}, u32[]{:S(2)}, u32[]{:S(2)}) collective-permute-start(f32[8,8,128]{2,1,0:T(8,128)S(1)} %add.3.mine), channel_id=1, source_target_pairs={{0,4},{1,5},{2,6},{3,7},{4,0},{5,1},{6,2},{7,3},{8,12},{9,13},{10,... | collective-permute-start | bytes 98312 | tf_op jit(solution)/shard_map/ppermute | solution.py:24
  23.6 3.4 %collective-permute-done.3.theirs = f32[8,8,128]{2,1,0:T(8,128)S(1)} collective-permute-done((f32[8,8,128]{2,1,0:T(8,128)S(1)}, f32[8,8,128]{2,1,0:T(8,128)S(1)}, u32[]{:S(2)}, u32[]{:S(2)}) %collective-permute-start.3) | collective-permute-done | bytes 32800 | tf_op jit(solution)/shard_map/ppermute | solution.py:24
  26.9 0.2 shard_map.81
  27.1 0.0 collective-permute-start.4
  27.1 1.4 %collective-permute-start.5 = (f32[8,128]{1,0:T(8,128)S(1)}, f32[8,128]{1,0:T(8,128)S(1)}, u32[]{:S(2)}, u32[]{:S(2)}) collective-permute-start(f32[8,128]{1,0:T(8,128)S(1)} %get-tuple-element.15.refs_3_), channel_id=1, source_target_pairs={{0,16},{8,24},{16,0},{24,8},{1,17},{9,25},{17,1},{25,9},{2,18},{10... | collective-permute-start | bytes 12296 | tf_op jit(solution)/shard_map/ppermute | solution.py:14
  28.5 0.5 %collective-permute-start.6 = (f32[8,128]{1,0:T(8,128)S(1)}, f32[8,128]{1,0:T(8,128)S(1)}, u32[]{:S(2)}, u32[]{:S(2)}) collective-permute-start(f32[8,128]{1,0:T(8,128)S(1)} %get-tuple-element.15.refs_3_), channel_id=1, source_target_pairs={{0,8},{8,0},{16,24},{24,16},{1,9},{9,1},{17,25},{25,17},{2,10},{10... | collective-permute-start | bytes 12296 | tf_op jit(solution)/shard_map/ppermute | solution.py:14
  29.0 1.2 %collective-permute-done.4.refs_0_ = f32[8,128]{1,0:T(8,128)S(1)} collective-permute-done((f32[8,128]{1,0:T(8,128)S(1)}, f32[8,128]{1,0:T(8,128)S(1)}, u32[]{:S(2)}, u32[]{:S(2)}) %collective-permute-start.4) | collective-permute-done | bytes 4128 | tf_op jit(solution)/shard_map/ppermute | solution.py:14
  30.2 0.6 %collective-permute-done.5.refs_1_ = f32[8,128]{1,0:T(8,128)S(1)} collective-permute-done((f32[8,128]{1,0:T(8,128)S(1)}, f32[8,128]{1,0:T(8,128)S(1)}, u32[]{:S(2)}, u32[]{:S(2)}) %collective-permute-start.5) | collective-permute-done | bytes 4128 | tf_op jit(solution)/shard_map/ppermute | solution.py:14
  30.8 0.0 collective-permute-done.6.refs_2_
  30.8 0.7 %shard_map.82 = (f32[1,8,128]{2,1,0:T(8,128)}, f32[1,8,128]{2,1,0:T(8,128)}, f32[8]{0:T(128)}) custom-call(f32[8,128]{1,0:T(8,128)S(1)} %collective-permute-done.4.refs_0_, f32[8,128]{1,0:T(8,128)S(1)} %collective-permute-done.5.refs_1_, f32[8,128]{1,0:T(8,128)S(1)} %collective-permute-done.6.refs_2_, f32[8,128]{1,0:T(8,128)S(1)} %get-tuple-element.15.refs_3_, ...), custom_call_target="tpu_custom_call" | custom-call | flops 10000 | bytes 100000 | tf_op jit(solution)/shard_map/pallas_call | solution.py:251
  (1 shorter events, 0.0 us)
Async XLA Ops:
  0.6 13.1 %collective-permute-start = (f32[8,1,128,128]{3,2,1,0:T(8,128)}, f32[8,1,128,128]{3,2,1,0:T(8,128)S(1)}, u32[]{:S(2)}, u32[]{:S(2)}) collective-permute-start(f32[8,1,128,128]{3,2,1,0:T(8,128)} %couplings.1), channel_id=1, source_target_pairs={{0,1},{1,0},{2,3},{3,2},{4,5},{5,4},{6,7},{7,6},{8,10},{9,11},{10,... | collective-permute-start | bytes 1572872 | tf_op jit(solution)/shard_map/ppermute | solution.py:24
  5.0 4.9 %copy-start.1 = (f32[10,128]{1,0:T(8,128)S(1)}, f32[10,128]{1,0:T(8,128)}, u32[]{:S(2)}) copy-start(f32[10,128]{1,0:T(8,128)} %get-tuple-element.13.side) | copy-start | bytes 15364
  5.0 12.7 %all-to-all-start = ((f32[32,8,128]{2,1,0:T(8,128)}), f32[32,8,128]{2,1,0:T(8,128)S(1)}, u32[]{:S(2)}, u32[]{:S(2)}) async-start(f32[32,8,128]{2,1,0:T(8,128)} %get-tuple-element.12), calls=%async_computation | async-start | bytes 262144 | tf_op jit(solution)/shard_map/all_to_all | solution.py:226
  10.0 3.7 %collective-permute-start.1 = (f32[10,128]{1,0:T(8,128)S(1)}, f32[10,128]{1,0:T(8,128)S(1)}, u32[]{:S(2)}, u32[]{:S(2)}) collective-permute-start(f32[10,128]{1,0:T(8,128)S(1)} %copy-done.1), channel_id=1, source_target_pairs={{0,1},{1,0},{2,3},{3,2},{4,5},{5,4},{6,7},{7,6},{8,10},{9,11},{10,... | collective-permute-start | bytes 15368 | tf_op jit(solution)/shard_map/ppermute | solution.py:24
  11.8 1.0 %copy-start = (f32[8,1,128,128]{3,2,1,0:T(8,128)S(1)}, f32[8,1,128,128]{3,2,1,0:T(8,128)}, u32[]{:S(2)}) copy-start(f32[8,1,128,128]{3,2,1,0:T(8,128)} %couplings.1) | copy-start | bytes 1572868
  18.1 4.0 %collective-permute-start.2 = (f32[8,8,128]{2,1,0:T(8,128)S(1)}, f32[8,8,128]{2,1,0:T(8,128)S(1)}, u32[]{:S(2)}, u32[]{:S(2)}) collective-permute-start(f32[8,8,128]{2,1,0:T(8,128)S(1)} %shard_map.79), channel_id=1, source_target_pairs={{0,2},{1,3},{2,0},{3,1},{4,6},{5,7},{6,4},{7,5},{8,9},{9,8},{10,11... | collective-permute-start | bytes 98312 | tf_op jit(solution)/shard_map/ppermute | solution.py:24
  22.1 4.8 %collective-permute-start.3 = (f32[8,8,128]{2,1,0:T(8,128)S(1)}, f32[8,8,128]{2,1,0:T(8,128)S(1)}, u32[]{:S(2)}, u32[]{:S(2)}) collective-permute-start(f32[8,8,128]{2,1,0:T(8,128)S(1)} %add.3.mine), channel_id=1, source_target_pairs={{0,4},{1,5},{2,6},{3,7},{4,0},{5,1},{6,2},{7,3},{8,12},{9,13},{10,... | collective-permute-start | bytes 98312 | tf_op jit(solution)/shard_map/ppermute | solution.py:24
  27.1 3.0 %collective-permute-start.4 = (f32[8,128]{1,0:T(8,128)S(1)}, f32[8,128]{1,0:T(8,128)S(1)}, u32[]{:S(2)}, u32[]{:S(2)}) collective-permute-start(f32[8,128]{1,0:T(8,128)S(1)} %get-tuple-element.15.refs_3_), channel_id=1, source_target_pairs={{0,24},{8,16},{16,8},{24,0},{1,25},{9,17},{17,9},{25,1},{2,26},{10... | collective-permute-start | bytes 12296 | tf_op jit(solution)/shard_map/ppermute | solution.py:14
  27.1 3.7 %collective-permute-start.5 = (f32[8,128]{1,0:T(8,128)S(1)}, f32[8,128]{1,0:T(8,128)S(1)}, u32[]{:S(2)}, u32[]{:S(2)}) collective-permute-start(f32[8,128]{1,0:T(8,128)S(1)} %get-tuple-element.15.refs_3_), channel_id=1, source_target_pairs={{0,16},{8,24},{16,0},{24,8},{1,17},{9,25},{17,1},{25,9},{2,18},{10... | collective-permute-start | bytes 12296 | tf_op jit(solution)/shard_map/ppermute | solution.py:14
  28.5 2.3 %collective-permute-start.6 = (f32[8,128]{1,0:T(8,128)S(1)}, f32[8,128]{1,0:T(8,128)S(1)}, u32[]{:S(2)}, u32[]{:S(2)}) collective-permute-start(f32[8,128]{1,0:T(8,128)S(1)} %get-tuple-element.15.refs_3_), channel_id=1, source_target_pairs={{0,8},{8,0},{16,24},{24,16},{1,9},{9,1},{17,25},{25,17},{2,10},{10... | collective-permute-start | bytes 12296 | tf_op jit(solution)/shard_map/ppermute | solution.py:14

commit v5 on v4

--- a/solution.py
+++ b/solution.py
@@ -171,7 +171,7 @@
     terms = jnp.where(lane == sublane + vectors, gram, 0.0) - jnp.where(
         lane < vectors, gram * mixing, 0.0
     )
-    totals = jnp.sum(terms, axis=1, keepdims=True)
+    totals = jnp.maximum(jnp.sum(terms, axis=1, keepdims=True), 0.0)
     column = jnp.sqrt(totals / solved[2 * vectors : 3 * vectors, :])
     norms[...] = jnp.sum(jnp.where(lane == sublane, column, 0.0), axis=0)[:vectors]
 

time: 31.7 us -> 31.7 us (level)
  no operation moved by 1% of the time
where the time goes in v5:
time: 31.7 us; the launch traced here: 31.5 us
  starting transfers between devices  14.2 us (45%)
  waiting for transfers between devices  11.6 us (37%)
  Pallas kernels  3.96 us (12%)
  local copies, waits for them, and re-layouts  1.05 us (3%)
  between operations  0.69 us (2%)
    ppermute x4, starting transfers between devices, pair(): return lax.ppermute(x, ('tgt', 'src'), partners)  7.36 us
    ppermute x4, waiting for transfers between devices, pair(): return lax.ppermute(x, ('tgt', 'src'), partners)  5.99 us
    all_to_all x1, starting transfers between devices, shards(): table = lax.all_to_all(copies, ('tgt', 'src'), 0, 0, tiled=True)  4.93 us
    all_to_all x1, waiting for transfers between devices, shards(): table = lax.all_to_all(copies, ('tgt', 'src'), 0, 0, tiled=True)  3.83 us
    ppermute x3, starting transfers between devices, exchange(): return lax.ppermute(x, axis, [(i, i ^ bit) for i in range(count)])  1.88 us
    ppermute x3, waiting for transfers between devices, exchange(): return lax.ppermute(x, axis, [(i, i ^ bit) for i in range(count)])  1.79 us
    pallas_call x1, Pallas kernels, shards(): pl.pallas_call(spread, out_shape=(shape(count, vectors, states), shape(*s...  1.38 us
    unnamed x4, local copies, waits for them, and re-layouts  1.05 us
  transfers between devices with their start and end apart: 8, of which 6 were waited for; matrix products, arithmetic and copies ran while one was open for 0% of the time, Pallas kernels for 8%

profile of v5, /device:TPU:0, one launch (start us, length us, event | category | flops | bytes accessed | tf_op | source)
XLA Modules:
  0.0 31.5 jit_solution(8544450547459451505)
XLA Ops:
  0.6 3.0 %collective-permute-start = (f32[8,1,128,128]{3,2,1,0:T(8,128)}, f32[8,1,128,128]{3,2,1,0:T(8,128)S(1)}, u32[]{:S(2)}, u32[]{:S(2)}) collective-permute-start(f32[8,1,128,128]{3,2,1,0:T(8,128)} %couplings.1), channel_id=1, source_target_pairs={{0,1},{1,0},{2,3},{3,2},{4,5},{5,4},{6,7},{7,6},{8,10},{9,11},{10,... | collective-permute-start | bytes 1572872 | tf_op jit(solution)/shard_map/ppermute | solution.py:24
  3.6 1.4 %shard_map.76 = (f32[32,8,128]{2,1,0:T(8,128)}, f32[10,128]{1,0:T(8,128)}) custom-call(f32[1,8,128]{2,1,0:T(8,128)} %bitcast.9, s32[1,8]{1,0:T(1,128)} %bitcast.10, s32[1,8]{1,0:T(1,128)} %bitcast.11, f32[1,128]{1,0:T(1,128)} %energies.1), custom_call_target="tpu_custom_call" | custom-call | tf_op jit(solution)/shard_map/pallas_call | solution.py:206
  5.0 0.0 copy-start.1
  5.0 4.9 %all-to-all-start = ((f32[32,8,128]{2,1,0:T(8,128)}), f32[32,8,128]{2,1,0:T(8,128)S(1)}, u32[]{:S(2)}, u32[]{:S(2)}) async-start(f32[32,8,128]{2,1,0:T(8,128)} %get-tuple-element.12), calls=%async_computation | async-start | bytes 262144 | tf_op jit(solution)/shard_map/all_to_all | solution.py:226
  10.0 0.0 copy-done.1
  10.0 1.8 %collective-permute-start.1 = (f32[10,128]{1,0:T(8,128)S(1)}, f32[10,128]{1,0:T(8,128)S(1)}, u32[]{:S(2)}, u32[]{:S(2)}) collective-permute-start(f32[10,128]{1,0:T(8,128)S(1)} %copy-done.1), channel_id=1, source_target_pairs={{0,1},{1,0},{2,3},{3,2},{4,5},{5,4},{6,7},{7,6},{8,10},{9,11},{10,... | collective-permute-start | bytes 15368 | tf_op jit(solution)/shard_map/ppermute | solution.py:24
  11.8 0.0 copy-start
  11.8 1.0 %copy-done = f32[8,1,128,128]{3,2,1,0:T(8,128)S(1)} copy-done((f32[8,1,128,128]{3,2,1,0:T(8,128)S(1)}, f32[8,1,128,128]{3,2,1,0:T(8,128)}, u32[]{:S(2)}) %copy-start) | copy-done | bytes 524312
  12.9 0.2 shard_map.77.halves
  13.0 0.7 %collective-permute-done.1.side.other_side = f32[10,128]{1,0:T(8,128)S(1)} collective-permute-done((f32[10,128]{1,0:T(8,128)S(1)}, f32[10,128]{1,0:T(8,128)S(1)}, u32[]{:S(2)}, u32[]{:S(2)}) %collective-permute-start.1) | collective-permute-done | bytes 5152 | tf_op jit(solution)/shard_map/ppermute | solution.py:24
  13.7 0.0 collective-permute-done.couplings
  13.7 0.2 shard_map.78.other_halves
  13.9 3.8 %all-to-all-done.table = f32[32,8,128]{2,1,0:T(8,128)S(1)} async-done(((f32[32,8,128]{2,1,0:T(8,128)}), f32[32,8,128]{2,1,0:T(8,128)S(1)}, u32[]{:S(2)}, u32[]{:S(2)}) %all-to-all-start) | async-done | bytes 131104 | tf_op jit(solution)/shard_map/all_to_all | solution.py:226
  17.7 0.4 %shard_map.79 = f32[8,8,128]{2,1,0:T(8,128)S(1)} custom-call(f32[32,8,128]{2,1,0:T(8,128)S(1)} %all-to-all-done.table, bf16[8,1,256,128]{3,2,1,0:T(8,128)(2,1)S(1)} %shard_map.77.halves, f32[10,128]{1,0:T(8,128)S(1)} %copy-done.1, bf16[8,1,256,128]{3,2,1,0:T(8,128)(2,1)S(1)} %shard_map.78.other_halves, f32[10,128]{1,0:T(8,128)S(1)} %collective-permute-done.1.side.other_side), custom_call_target="tpu_custom_call" | custom-call | flops 4194304 | bytes 1048576 | tf_op jit(solution)/shard_map/pallas_call | solution.py:227
  18.1 1.1 %collective-permute-start.2 = (f32[8,8,128]{2,1,0:T(8,128)S(1)}, f32[8,8,128]{2,1,0:T(8,128)S(1)}, u32[]{:S(2)}, u32[]{:S(2)}) collective-permute-start(f32[8,8,128]{2,1,0:T(8,128)S(1)} %shard_map.79), channel_id=1, source_target_pairs={{0,2},{1,3},{2,0},{3,1},{4,6},{5,7},{6,4},{7,5},{8,9},{9,8},{10,11... | collective-permute-start | bytes 98312 | tf_op jit(solution)/shard_map/ppermute | solution.py:24
  19.2 0.9 %shard_map.80.refs_4_ = f32[24,128]{1,0:T(8,128)S(1)} custom-call(f32[32,8,128]{2,1,0:T(8,128)S(1)} %all-to-all-done.table), custom_call_target="tpu_custom_call" | custom-call | flops 1000000 | bytes 131072 | tf_op jit(solution)/shard_map/pallas_call | solution.py:230
  20.2 2.0 %collective-permute-done.2 = f32[8,8,128]{2,1,0:T(8,128)S(1)} collective-permute-done((f32[8,8,128]{2,1,0:T(8,128)S(1)}, f32[8,8,128]{2,1,0:T(8,128)S(1)}, u32[]{:S(2)}, u32[]{:S(2)}) %collective-permute-start.2) | collective-permute-done | bytes 32800 | tf_op jit(solution)/shard_map/ppermute | solution.py:24
  22.1 1.4 %collective-permute-start.3 = (f32[8,8,128]{2,1,0:T(8,128)S(1)}, f32[8,8,128]{2,1,0:T(8,128)S(1)}, u32[]{:S(2)}, u32[]{:S(2)}) collective-permute-start(f32[8,8,128]{2,1,0:T(8,128)S(1)} %add.3.mine), channel_id=1, source_target_pairs={{0,4},{1,5},{2,6},{3,7},{4,0},{5,1},{6,2},{7,3},{8,12},{9,13},{10,... | collective-permute-start | bytes 98312 | tf_op jit(solution)/shard_map/ppermute | solution.py:24
  23.6 3.4 %collective-permute-done.3.theirs = f32[8,8,128]{2,1,0:T(8,128)S(1)} collective-permute-done((f32[8,8,128]{2,1,0:T(8,128)S(1)}, f32[8,8,128]{2,1,0:T(8,128)S(1)}, u32[]{:S(2)}, u32[]{:S(2)}) %collective-permute-start.3) | collective-permute-done | bytes 32800 | tf_op jit(solution)/shard_map/ppermute | solution.py:24
  26.9 0.2 shard_map.81
  27.1 0.0 collective-permute-start.4
  27.1 1.4 %collective-permute-start.5 = (f32[8,128]{1,0:T(8,128)S(1)}, f32[8,128]{1,0:T(8,128)S(1)}, u32[]{:S(2)}, u32[]{:S(2)}) collective-permute-start(f32[8,128]{1,0:T(8,128)S(1)} %get-tuple-element.15.refs_3_), channel_id=1, source_target_pairs={{0,16},{8,24},{16,0},{24,8},{1,17},{9,25},{17,1},{25,9},{2,18},{10... | collective-permute-start | bytes 12296 | tf_op jit(solution)/shard_map/ppermute | solution.py:14
  28.5 0.5 %collective-permute-start.6 = (f32[8,128]{1,0:T(8,128)S(1)}, f32[8,128]{1,0:T(8,128)S(1)}, u32[]{:S(2)}, u32[]{:S(2)}) collective-permute-start(f32[8,128]{1,0:T(8,128)S(1)} %get-tuple-element.15.refs_3_), channel_id=1, source_target_pairs={{0,8},{8,0},{16,24},{24,16},{1,9},{9,1},{17,25},{25,17},{2,10},{10... | collective-permute-start | bytes 12296 | tf_op jit(solution)/shard_map/ppermute | solution.py:14
  29.0 1.2 %collective-permute-done.4.refs_0_ = f32[8,128]{1,0:T(8,128)S(1)} collective-permute-done((f32[8,128]{1,0:T(8,128)S(1)}, f32[8,128]{1,0:T(8,128)S(1)}, u32[]{:S(2)}, u32[]{:S(2)}) %collective-permute-start.4) | collective-permute-done | bytes 4128 | tf_op jit(solution)/shard_map/ppermute | solution.py:14
  30.2 0.6 %collective-permute-done.5.refs_1_ = f32[8,128]{1,0:T(8,128)S(1)} collective-permute-done((f32[8,128]{1,0:T(8,128)S(1)}, f32[8,128]{1,0:T(8,128)S(1)}, u32[]{:S(2)}, u32[]{:S(2)}) %collective-permute-start.5) | collective-permute-done | bytes 4128 | tf_op jit(solution)/shard_map/ppermute | solution.py:14
  30.8 0.0 collective-permute-done.6.refs_2_
  30.8 0.7 %shard_map.82 = (f32[1,8,128]{2,1,0:T(8,128)}, f32[1,8,128]{2,1,0:T(8,128)}, f32[8]{0:T(128)}) custom-call(f32[8,128]{1,0:T(8,128)S(1)} %collective-permute-done.4.refs_0_, f32[8,128]{1,0:T(8,128)S(1)} %collective-permute-done.5.refs_1_, f32[8,128]{1,0:T(8,128)S(1)} %collective-permute-done.6.refs_2_, f32[8,128]{1,0:T(8,128)S(1)} %get-tuple-element.15.refs_3_, ...), custom_call_target="tpu_custom_call" | custom-call | flops 10000 | bytes 100000 | tf_op jit(solution)/shard_map/pallas_call | solution.py:251
  (1 shorter events, 0.0 us)
Async XLA Ops:
  0.6 13.1 %collective-permute-start = (f32[8,1,128,128]{3,2,1,0:T(8,128)}, f32[8,1,128,128]{3,2,1,0:T(8,128)S(1)}, u32[]{:S(2)}, u32[]{:S(2)}) collective-permute-start(f32[8,1,128,128]{3,2,1,0:T(8,128)} %couplings.1), channel_id=1, source_target_pairs={{0,1},{1,0},{2,3},{3,2},{4,5},{5,4},{6,7},{7,6},{8,10},{9,11},{10,... | collective-permute-start | bytes 1572872 | tf_op jit(solution)/shard_map/ppermute | solution.py:24
  5.0 4.9 %copy-start.1 = (f32[10,128]{1,0:T(8,128)S(1)}, f32[10,128]{1,0:T(8,128)}, u32[]{:S(2)}) copy-start(f32[10,128]{1,0:T(8,128)} %get-tuple-element.13.side) | copy-start | bytes 15364
  5.0 12.7 %all-to-all-start = ((f32[32,8,128]{2,1,0:T(8,128)}), f32[32,8,128]{2,1,0:T(8,128)S(1)}, u32[]{:S(2)}, u32[]{:S(2)}) async-start(f32[32,8,128]{2,1,0:T(8,128)} %get-tuple-element.12), calls=%async_computation | async-start | bytes 262144 | tf_op jit(solution)/shard_map/all_to_all | solution.py:226
  10.0 3.7 %collective-permute-start.1 = (f32[10,128]{1,0:T(8,128)S(1)}, f32[10,128]{1,0:T(8,128)S(1)}, u32[]{:S(2)}, u32[]{:S(2)}) collective-permute-start(f32[10,128]{1,0:T(8,128)S(1)} %copy-done.1), channel_id=1, source_target_pairs={{0,1},{1,0},{2,3},{3,2},{4,5},{5,4},{6,7},{7,6},{8,10},{9,11},{10,... | collective-permute-start | bytes 15368 | tf_op jit(solution)/shard_map/ppermute | solution.py:24
  11.8 1.0 %copy-start = (f32[8,1,128,128]{3,2,1,0:T(8,128)S(1)}, f32[8,1,128,128]{3,2,1,0:T(8,128)}, u32[]{:S(2)}) copy-start(f32[8,1,128,128]{3,2,1,0:T(8,128)} %couplings.1) | copy-start | bytes 1572868
  18.1 4.0 %collective-permute-start.2 = (f32[8,8,128]{2,1,0:T(8,128)S(1)}, f32[8,8,128]{2,1,0:T(8,128)S(1)}, u32[]{:S(2)}, u32[]{:S(2)}) collective-permute-start(f32[8,8,128]{2,1,0:T(8,128)S(1)} %shard_map.79), channel_id=1, source_target_pairs={{0,2},{1,3},{2,0},{3,1},{4,6},{5,7},{6,4},{7,5},{8,9},{9,8},{10,11... | collective-permute-start | bytes 98312 | tf_op jit(solution)/shard_map/ppermute | solution.py:24
  22.1 4.8 %collective-permute-start.3 = (f32[8,8,128]{2,1,0:T(8,128)S(1)}, f32[8,8,128]{2,1,0:T(8,128)S(1)}, u32[]{:S(2)}, u32[]{:S(2)}) collective-permute-start(f32[8,8,128]{2,1,0:T(8,128)S(1)} %add.3.mine), channel_id=1, source_target_pairs={{0,4},{1,5},{2,6},{3,7},{4,0},{5,1},{6,2},{7,3},{8,12},{9,13},{10,... | collective-permute-start | bytes 98312 | tf_op jit(solution)/shard_map/ppermute | solution.py:24
  27.1 3.0 %collective-permute-start.4 = (f32[8,128]{1,0:T(8,128)S(1)}, f32[8,128]{1,0:T(8,128)S(1)}, u32[]{:S(2)}, u32[]{:S(2)}) collective-permute-start(f32[8,128]{1,0:T(8,128)S(1)} %get-tuple-element.15.refs_3_), channel_id=1, source_target_pairs={{0,24},{8,16},{16,8},{24,0},{1,25},{9,17},{17,9},{25,1},{2,26},{10... | collective-permute-start | bytes 12296 | tf_op jit(solution)/shard_map/ppermute | solution.py:14
  27.1 3.7 %collective-permute-start.5 = (f32[8,128]{1,0:T(8,128)S(1)}, f32[8,128]{1,0:T(8,128)S(1)}, u32[]{:S(2)}, u32[]{:S(2)}) collective-permute-start(f32[8,128]{1,0:T(8,128)S(1)} %get-tuple-element.15.refs_3_), channel_id=1, source_target_pairs={{0,16},{8,24},{16,0},{24,8},{1,17},{9,25},{17,1},{25,9},{2,18},{10... | collective-permute-start | bytes 12296 | tf_op jit(solution)/shard_map/ppermute | solution.py:14
  28.5 2.3 %collective-permute-start.6 = (f32[8,128]{1,0:T(8,128)S(1)}, f32[8,128]{1,0:T(8,128)S(1)}, u32[]{:S(2)}, u32[]{:S(2)}) collective-permute-start(f32[8,128]{1,0:T(8,128)S(1)} %get-tuple-element.15.refs_3_), channel_id=1, source_target_pairs={{0,8},{8,0},{16,24},{24,16},{1,9},{9,1},{17,25},{25,17},{2,10},{10... | collective-permute-start | bytes 12296 | tf_op jit(solution)/shard_map/ppermute | solution.py:14

commit v6 on v5

--- a/solution.py
+++ b/solution.py
@@ -138,10 +138,10 @@
     out[2 * vectors : 3 * vectors] = jnp.broadcast_to(diagonal, (vectors, states))
 
 
-def grams(mine, theirs, table, own, gram, sigmas):
+def grams(mine, near, far, both, table, own, gram, sigmas):
     targets, vectors, states = mine.shape
     first = lax.axis_index("tgt") * targets
-    sigmas[...] = mine[...] + theirs[...]
+    sigmas[...] = (mine[...] + near[...]) + (far[...] + both[...])
     own[...] = sigmas[lax.axis_index("src")]
     block = jnp.concatenate([table[first + i] for i in range(targets)], axis=1)
     wide = jnp.concatenate([sigmas[i] for i in range(targets)], axis=1)
@@ -229,20 +229,21 @@
     )(table, halves, side, other_halves, other_side)
     solved = call(invert, shape(3 * vectors, states), [VMEM], 10**6, 4 * table.size)(table)
 
-    steps = [(2, 1)] + [(bit, bit) for bit in bits_of(src_count)[2:]]
-    for n, step in enumerate(steps):
-        theirs = pair(partial, step)
-        if n + 1 < len(steps):
-            partial = partial + theirs
-            partial, solved = lax.optimization_barrier((partial, solved))
+    steps = [(bit, bit) for bit in bits_of(src_count)[2:]]
+    for step in steps[1:]:
+        partial = partial + pair(partial, step)
+    near, far = (2, 1), steps[0]
+    both = (near[0] ^ far[0], near[1] ^ far[1])
+    parts = [pair(partial, step) for step in (near, far, both)]
+    parts = [parts[n] for n in (0, 1, 2)]
     own, gram = call(
         grams,
         (shape(vectors, states), shape(vectors, states)),
-        [VMEM] * 3,
+        [VMEM] * 5,
         10**6,
         12 * partial.size,
         [pltpu.VMEM((targets, vectors, states), jnp.float32)],
-    )(partial, theirs, table)
+    )(partial, *parts, table)
 
     for bit in reversed(bits_of(tgt_count)[2:]):
         gram = gram + exchange(gram, "tgt", bit)

time: 31.7 us -> 30.7 us (0.968)
  waiting for transfers between devices: 11.6 us -> 8.67 us
  starting transfers between devices: 14.2 us -> 16.1 us
    ppermute x4 -> x5, waiting for transfers between devices: 5.99 us -> 3.99 us  [pair(): return lax.ppermute(x, ('tgt', 'src'), partners)]
    ppermute x4 -> x5, starting transfers between devices: 7.36 us -> 9.28 us  [pair(): return lax.ppermute(x, ('tgt', 'src'), partners)]
    ppermute x3, waiting for transfers between devices: 1.79 us -> 0.84 us  [exchange(): return lax.ppermute(x, axis, [(i, i ^ bit) for i in range(count)])]
  transfers between devices with their start and end apart: 8 -> 9, of which waited for: 6 -> 6; matrix products, arithmetic and copies ran while one was open for 0% -> 0% of each run, Pallas kernels for 8% -> 9%
where the time goes in v6:
time: 30.7 us; the launch traced here: 30.5 us
  starting transfers between devices  16.1 us (52%)
  waiting for transfers between devices  8.67 us (28%)
  Pallas kernels  3.97 us (13%)
  local copies, waits for them, and re-layouts  1.05 us (3%)
  between operations  0.69 us (2%)
    ppermute x5, starting transfers between devices, pair(): return lax.ppermute(x, ('tgt', 'src'), partners)  9.28 us
    all_to_all x1, starting transfers between devices, shards(): table = lax.all_to_all(copies, ('tgt', 'src'), 0, 0, tiled=True)  4.93 us
    ppermute x5, waiting for transfers between devices, pair(): return lax.ppermute(x, ('tgt', 'src'), partners)  3.99 us
    all_to_all x1, waiting for transfers between devices, shards(): table = lax.all_to_all(copies, ('tgt', 'src'), 0, 0, tiled=True)  3.83 us
    ppermute x3, starting transfers between devices, exchange(): return lax.ppermute(x, axis, [(i, i ^ bit) for i in range(count)])  1.88 us
    pallas_call x1, Pallas kernels, shards(): pl.pallas_call(spread, out_shape=(shape(count, vectors, states), shape(*s...  1.39 us
    unnamed x4, local copies, waits for them, and re-layouts  1.05 us
    pallas_call x1, Pallas kernels, shards(): call(invert, shape(3 * vectors, states), [VMEM], 10 ** 6, 4 * table.size)  0.95 us
  transfers between devices with their start and end apart: 9, of which 6 were waited for; matrix products, arithmetic and copies ran while one was open for 0% of the time, Pallas kernels for 9%

profile of v6, /device:TPU:0, one launch (start us, length us, event | category | flops | bytes accessed | tf_op | source)
XLA Modules:
  0.0 30.5 jit_solution(9627187830667056373)
XLA Ops:
  0.6 3.0 %collective-permute-start = (f32[8,1,128,128]{3,2,1,0:T(8,128)}, f32[8,1,128,128]{3,2,1,0:T(8,128)S(1)}, u32[]{:S(2)}, u32[]{:S(2)}) collective-permute-start(f32[8,1,128,128]{3,2,1,0:T(8,128)} %couplings.1), channel_id=1, source_target_pairs={{0,1},{1,0},{2,3},{3,2},{4,5},{5,4},{6,7},{7,6},{8,10},{9,11},{10,... | collective-permute-start | bytes 1572872 | tf_op jit(solution)/shard_map/ppermute | solution.py:24
  3.6 1.4 %shard_map.76 = (f32[32,8,128]{2,1,0:T(8,128)}, f32[10,128]{1,0:T(8,128)}) custom-call(f32[1,8,128]{2,1,0:T(8,128)} %bitcast.9, s32[1,8]{1,0:T(1,128)} %bitcast.10, s32[1,8]{1,0:T(1,128)} %bitcast.11, f32[1,128]{1,0:T(1,128)} %energies.1), custom_call_target="tpu_custom_call" | custom-call | tf_op jit(solution)/shard_map/pallas_call | solution.py:206
  5.0 0.0 copy-start.1
  5.0 4.9 %all-to-all-start = ((f32[32,8,128]{2,1,0:T(8,128)}), f32[32,8,128]{2,1,0:T(8,128)S(1)}, u32[]{:S(2)}, u32[]{:S(2)}) async-start(f32[32,8,128]{2,1,0:T(8,128)} %get-tuple-element.10), calls=%async_computation | async-start | bytes 262144 | tf_op jit(solution)/shard_map/all_to_all | solution.py:226
  10.0 0.0 copy-done.1
  10.0 1.8 %collective-permute-start.1 = (f32[10,128]{1,0:T(8,128)S(1)}, f32[10,128]{1,0:T(8,128)S(1)}, u32[]{:S(2)}, u32[]{:S(2)}) collective-permute-start(f32[10,128]{1,0:T(8,128)S(1)} %copy-done.1), channel_id=1, source_target_pairs={{0,1},{1,0},{2,3},{3,2},{4,5},{5,4},{6,7},{7,6},{8,10},{9,11},{10,... | collective-permute-start | bytes 15368 | tf_op jit(solution)/shard_map/ppermute | solution.py:24
  11.8 0.0 copy-start
  11.8 1.0 %copy-done = f32[8,1,128,128]{3,2,1,0:T(8,128)S(1)} copy-done((f32[8,1,128,128]{3,2,1,0:T(8,128)S(1)}, f32[8,1,128,128]{3,2,1,0:T(8,128)}, u32[]{:S(2)}) %copy-start) | copy-done | bytes 524312
  12.9 0.2 shard_map.77.halves
  13.0 0.7 %collective-permute-done.1.side.other_side = f32[10,128]{1,0:T(8,128)S(1)} collective-permute-done((f32[10,128]{1,0:T(8,128)S(1)}, f32[10,128]{1,0:T(8,128)S(1)}, u32[]{:S(2)}, u32[]{:S(2)}) %collective-permute-start.1) | collective-permute-done | bytes 5152 | tf_op jit(solution)/shard_map/ppermute | solution.py:24
  13.7 0.0 collective-permute-done.couplings
  13.7 0.2 shard_map.78.other_halves
  13.9 3.8 %all-to-all-done.table = f32[32,8,128]{2,1,0:T(8,128)S(1)} async-done(((f32[32,8,128]{2,1,0:T(8,128)}), f32[32,8,128]{2,1,0:T(8,128)S(1)}, u32[]{:S(2)}, u32[]{:S(2)}) %all-to-all-start) | async-done | bytes 131104 | tf_op jit(solution)/shard_map/all_to_all | solution.py:226
  17.7 0.4 %shard_map.79.mine = f32[8,8,128]{2,1,0:T(8,128)S(1)} custom-call(f32[32,8,128]{2,1,0:T(8,128)S(1)} %all-to-all-done.table, bf16[8,1,256,128]{3,2,1,0:T(8,128)(2,1)S(1)} %shard_map.77.halves, f32[10,128]{1,0:T(8,128)S(1)} %copy-done.1, bf16[8,1,256,128]{3,2,1,0:T(8,128)(2,1)S(1)} %shard_map.78.other_halves, f32[10,128]{1,0:T(8,128)S(1)} %collective-permute-done.1.side.other_side), custom_call_target="tpu_custom_call" | custom-call | flops 4194304 | bytes 1048576 | tf_op jit(solution)/shard_map/pallas_call | solution.py:227
  18.1 1.1 %collective-permute-start.2 = (f32[8,8,128]{2,1,0:T(8,128)S(1)}, f32[8,8,128]{2,1,0:T(8,128)S(1)}, u32[]{:S(2)}, u32[]{:S(2)}) collective-permute-start(f32[8,8,128]{2,1,0:T(8,128)S(1)} %shard_map.79.mine), channel_id=1, source_target_pairs={{0,2},{1,3},{2,0},{3,1},{4,6},{5,7},{6,4},{7,5},{8,9},{9,8},{10,11... | collective-permute-start | bytes 98312 | tf_op jit(solution)/shard_map/ppermute | solution.py:24
  19.2 1.0 %collective-permute-start.3 = (f32[8,8,128]{2,1,0:T(8,128)S(1)}, f32[8,8,128]{2,1,0:T(8,128)S(1)}, u32[]{:S(2)}, u32[]{:S(2)}) collective-permute-start(f32[8,8,128]{2,1,0:T(8,128)S(1)} %shard_map.79.mine), channel_id=1, source_target_pairs={{0,4},{1,5},{2,6},{3,7},{4,0},{5,1},{6,2},{7,3},{8,12},{9,13},{10,... | collective-permute-start | bytes 98312 | tf_op jit(solution)/shard_map/ppermute | solution.py:24
  20.2 2.4 %collective-permute-start.4 = (f32[8,8,128]{2,1,0:T(8,128)S(1)}, f32[8,8,128]{2,1,0:T(8,128)S(1)}, u32[]{:S(2)}, u32[]{:S(2)}) collective-permute-start(f32[8,8,128]{2,1,0:T(8,128)S(1)} %shard_map.79.mine), channel_id=1, source_target_pairs={{0,6},{1,7},{2,4},{3,5},{4,2},{5,3},{6,0},{7,1},{8,13},{9,12},{10,... | collective-permute-start | bytes 98312 | tf_op jit(solution)/shard_map/ppermute | solution.py:24
  22.6 0.0 collective-permute-done.2.near
  22.6 2.4 %collective-permute-done.3.far = f32[8,8,128]{2,1,0:T(8,128)S(1)} collective-permute-done((f32[8,8,128]{2,1,0:T(8,128)S(1)}, f32[8,8,128]{2,1,0:T(8,128)S(1)}, u32[]{:S(2)}, u32[]{:S(2)}) %collective-permute-start.3) | collective-permute-done | bytes 32800 | tf_op jit(solution)/shard_map/ppermute | solution.py:24
  25.0 0.9 %collective-permute-done.4.both = f32[8,8,128]{2,1,0:T(8,128)S(1)} collective-permute-done((f32[8,8,128]{2,1,0:T(8,128)S(1)}, f32[8,8,128]{2,1,0:T(8,128)S(1)}, u32[]{:S(2)}, u32[]{:S(2)}) %collective-permute-start.4) | collective-permute-done | bytes 32800 | tf_op jit(solution)/shard_map/ppermute | solution.py:24
  25.9 0.2 shard_map.80
  26.1 0.0 collective-permute-start.5
  26.1 1.3 %collective-permute-start.6 = (f32[8,128]{1,0:T(8,128)S(1)}, f32[8,128]{1,0:T(8,128)S(1)}, u32[]{:S(2)}, u32[]{:S(2)}) collective-permute-start(f32[8,128]{1,0:T(8,128)S(1)} %get-tuple-element.12.refs_3_), channel_id=1, source_target_pairs={{0,16},{8,24},{16,0},{24,8},{1,17},{9,25},{17,1},{25,9},{2,18},{10... | collective-permute-start | bytes 12296 | tf_op jit(solution)/shard_map/ppermute | solution.py:14
  27.4 0.6 %collective-permute-start.7 = (f32[8,128]{1,0:T(8,128)S(1)}, f32[8,128]{1,0:T(8,128)S(1)}, u32[]{:S(2)}, u32[]{:S(2)}) collective-permute-start(f32[8,128]{1,0:T(8,128)S(1)} %get-tuple-element.12.refs_3_), channel_id=1, source_target_pairs={{0,8},{8,0},{16,24},{24,16},{1,9},{9,1},{17,25},{25,17},{2,10},{10... | collective-permute-start | bytes 12296 | tf_op jit(solution)/shard_map/ppermute | solution.py:14
  28.0 0.9 %shard_map.81.refs_4_ = f32[24,128]{1,0:T(8,128)S(1)} custom-call(f32[32,8,128]{2,1,0:T(8,128)S(1)} %all-to-all-done.table), custom_call_target="tpu_custom_call" | custom-call | flops 1000000 | bytes 131072 | tf_op jit(solution)/shard_map/pallas_call | solution.py:230
  28.9 0.2 collective-permute-done.5.refs_0_
  29.1 0.6 %collective-permute-done.6.refs_1_ = f32[8,128]{1,0:T(8,128)S(1)} collective-permute-done((f32[8,128]{1,0:T(8,128)S(1)}, f32[8,128]{1,0:T(8,128)S(1)}, u32[]{:S(2)}, u32[]{:S(2)}) %collective-permute-start.6) | collective-permute-done | bytes 4128 | tf_op jit(solution)/shard_map/ppermute | solution.py:14
  29.8 0.0 collective-permute-done.7.refs_2_
  29.8 0.7 %shard_map.82 = (f32[1,8,128]{2,1,0:T(8,128)}, f32[1,8,128]{2,1,0:T(8,128)}, f32[8]{0:T(128)}) custom-call(f32[8,128]{1,0:T(8,128)S(1)} %collective-permute-done.5.refs_0_, f32[8,128]{1,0:T(8,128)S(1)} %collective-permute-done.6.refs_1_, f32[8,128]{1,0:T(8,128)S(1)} %collective-permute-done.7.refs_2_, f32[8,128]{1,0:T(8,128)S(1)} %get-tuple-element.12.refs_3_, ...), custom_call_target="tpu_custom_call" | custom-call | flops 10000 | bytes 100000 | tf_op jit(solution)/shard_map/pallas_call | solution.py:252
Async XLA Ops:
  0.6 13.1 %collective-permute-start = (f32[8,1,128,128]{3,2,1,0:T(8,128)}, f32[8,1,128,128]{3,2,1,0:T(8,128)S(1)}, u32[]{:S(2)}, u32[]{:S(2)}) collective-permute-start(f32[8,1,128,128]{3,2,1,0:T(8,128)} %couplings.1), channel_id=1, source_target_pairs={{0,1},{1,0},{2,3},{3,2},{4,5},{5,4},{6,7},{7,6},{8,10},{9,11},{10,... | collective-permute-start | bytes 1572872 | tf_op jit(solution)/shard_map/ppermute | solution.py:24
  5.0 4.9 %copy-start.1 = (f32[10,128]{1,0:T(8,128)S(1)}, f32[10,128]{1,0:T(8,128)}, u32[]{:S(2)}) copy-start(f32[10,128]{1,0:T(8,128)} %get-tuple-element.11.side) | copy-start | bytes 15364
  5.0 12.7 %all-to-all-start = ((f32[32,8,128]{2,1,0:T(8,128)}), f32[32,8,128]{2,1,0:T(8,128)S(1)}, u32[]{:S(2)}, u32[]{:S(2)}) async-start(f32[32,8,128]{2,1,0:T(8,128)} %get-tuple-element.10), calls=%async_computation | async-start | bytes 262144 | tf_op jit(solution)/shard_map/all_to_all | solution.py:226
  10.0 3.7 %collective-permute-start.1 = (f32[10,128]{1,0:T(8,128)S(1)}, f32[10,128]{1,0:T(8,128)S(1)}, u32[]{:S(2)}, u32[]{:S(2)}) collective-permute-start(f32[10,128]{1,0:T(8,128)S(1)} %copy-done.1), channel_id=1, source_target_pairs={{0,1},{1,0},{2,3},{3,2},{4,5},{5,4},{6,7},{7,6},{8,10},{9,11},{10,... | collective-permute-start | bytes 15368 | tf_op jit(solution)/shard_map/ppermute | solution.py:24
  11.8 1.0 %copy-start = (f32[8,1,128,128]{3,2,1,0:T(8,128)S(1)}, f32[8,1,128,128]{3,2,1,0:T(8,128)}, u32[]{:S(2)}) copy-start(f32[8,1,128,128]{3,2,1,0:T(8,128)} %couplings.1) | copy-start | bytes 1572868
  18.1 4.5 %collective-permute-start.2 = (f32[8,8,128]{2,1,0:T(8,128)S(1)}, f32[8,8,128]{2,1,0:T(8,128)S(1)}, u32[]{:S(2)}, u32[]{:S(2)}) collective-permute-start(f32[8,8,128]{2,1,0:T(8,128)S(1)} %shard_map.79.mine), channel_id=1, source_target_pairs={{0,2},{1,3},{2,0},{3,1},{4,6},{5,7},{6,4},{7,5},{8,9},{9,8},{10,11... | collective-permute-start | bytes 98312 | tf_op jit(solution)/shard_map/ppermute | solution.py:24
  19.2 5.8 %collective-permute-start.3 = (f32[8,8,128]{2,1,0:T(8,128)S(1)}, f32[8,8,128]{2,1,0:T(8,128)S(1)}, u32[]{:S(2)}, u32[]{:S(2)}) collective-permute-start(f32[8,8,128]{2,1,0:T(8,128)S(1)} %shard_map.79.mine), channel_id=1, source_target_pairs={{0,4},{1,5},{2,6},{3,7},{4,0},{5,1},{6,2},{7,3},{8,12},{9,13},{10,... | collective-permute-start | bytes 98312 | tf_op jit(solution)/shard_map/ppermute | solution.py:24
  20.2 5.7 %collective-permute-start.4 = (f32[8,8,128]{2,1,0:T(8,128)S(1)}, f32[8,8,128]{2,1,0:T(8,128)S(1)}, u32[]{:S(2)}, u32[]{:S(2)}) collective-permute-start(f32[8,8,128]{2,1,0:T(8,128)S(1)} %shard_map.79.mine), channel_id=1, source_target_pairs={{0,6},{1,7},{2,4},{3,5},{4,2},{5,3},{6,0},{7,1},{8,13},{9,12},{10,... | collective-permute-start | bytes 98312 | tf_op jit(solution)/shard_map/ppermute | solution.py:24
  26.1 3.0 %collective-permute-start.5 = (f32[8,128]{1,0:T(8,128)S(1)}, f32[8,128]{1,0:T(8,128)S(1)}, u32[]{:S(2)}, u32[]{:S(2)}) collective-permute-start(f32[8,128]{1,0:T(8,128)S(1)} %get-tuple-element.12.refs_3_), channel_id=1, source_target_pairs={{0,24},{8,16},{16,8},{24,0},{1,25},{9,17},{17,9},{25,1},{2,26},{10... | collective-permute-start | bytes 12296 | tf_op jit(solution)/shard_map/ppermute | solution.py:14
  26.1 3.7 %collective-permute-start.6 = (f32[8,128]{1,0:T(8,128)S(1)}, f32[8,128]{1,0:T(8,128)S(1)}, u32[]{:S(2)}, u32[]{:S(2)}) collective-permute-start(f32[8,128]{1,0:T(8,128)S(1)} %get-tuple-element.12.refs_3_), channel_id=1, source_target_pairs={{0,16},{8,24},{16,0},{24,8},{1,17},{9,25},{17,1},{25,9},{2,18},{10... | collective-permute-start | bytes 12296 | tf_op jit(solution)/shard_map/ppermute | solution.py:14
  27.4 2.4 %collective-permute-start.7 = (f32[8,128]{1,0:T(8,128)S(1)}, f32[8,128]{1,0:T(8,128)S(1)}, u32[]{:S(2)}, u32[]{:S(2)}) collective-permute-start(f32[8,128]{1,0:T(8,128)S(1)} %get-tuple-element.12.refs_3_), channel_id=1, source_target_pairs={{0,8},{8,0},{16,24},{24,16},{1,9},{9,1},{17,25},{25,17},{2,10},{10... | collective-permute-start | bytes 12296 | tf_op jit(solution)/shard_map/ppermute | solution.py:14

commit v7 on v6

--- a/solution.py
+++ b/solution.py
@@ -236,6 +236,7 @@
     both = (near[0] ^ far[0], near[1] ^ far[1])
     parts = [pair(partial, step) for step in (near, far, both)]
     parts = [parts[n] for n in (0, 1, 2)]
+    parts[0], solved = lax.optimization_barrier((parts[0], solved))
     own, gram = call(
         grams,
         (shape(vectors, states), shape(vectors, states)),

time: 30.7 us -> 30.7 us (level)
    ppermute x5, waiting for transfers between devices: 3.99 us -> 3.04 us  [pair(): return lax.ppermute(x, ('tgt', 'src'), partners)]
    ppermute x3, waiting for transfers between devices: 0.84 us -> 1.79 us  [exchange(): return lax.ppermute(x, axis, [(i, i ^ bit) for i in range(count)])]
where the time goes in v7:
time: 30.7 us; the launch traced here: 30.5 us
  starting transfers between devices  16.1 us (52%)
  waiting for transfers between devices  8.67 us (28%)
  Pallas kernels  3.97 us (13%)
  local copies, waits for them, and re-layouts  1.05 us (3%)
  between operations  0.69 us (2%)
    ppermute x5, starting transfers between devices, pair(): return lax.ppermute(x, ('tgt', 'src'), partners)  9.28 us
    all_to_all x1, starting transfers between devices, shards(): table = lax.all_to_all(copies, ('tgt', 'src'), 0, 0, tiled=True)  4.93 us
    all_to_all x1, waiting for transfers between devices, shards(): table = lax.all_to_all(copies, ('tgt', 'src'), 0, 0, tiled=True)  3.83 us
    ppermute x5, waiting for transfers between devices, pair(): return lax.ppermute(x, ('tgt', 'src'), partners)  3.04 us
    ppermute x3, starting transfers between devices, exchange(): return lax.ppermute(x, axis, [(i, i ^ bit) for i in range(count)])  1.88 us
    ppermute x3, waiting for transfers between devices, exchange(): return lax.ppermute(x, axis, [(i, i ^ bit) for i in range(count)])  1.79 us
    pallas_call x1, Pallas kernels, shards(): pl.pallas_call(spread, out_shape=(shape(count, vectors, states), shape(*s...  1.39 us
    unnamed x4, local copies, waits for them, and re-layouts  1.05 us
  transfers between devices with their start and end apart: 9, of which 6 were waited for; matrix products, arithmetic and copies ran while one was open for 0% of the time, Pallas kernels for 9%

profile of v7, /device:TPU:0, one launch (start us, length us, event | category | flops | bytes accessed | tf_op | source)
XLA Modules:
  0.0 30.5 jit_solution(4238203085704125141)
XLA Ops:
  0.6 3.0 %collective-permute-start = (f32[8,1,128,128]{3,2,1,0:T(8,128)}, f32[8,1,128,128]{3,2,1,0:T(8,128)S(1)}, u32[]{:S(2)}, u32[]{:S(2)}) collective-permute-start(f32[8,1,128,128]{3,2,1,0:T(8,128)} %couplings.1), channel_id=1, source_target_pairs={{0,1},{1,0},{2,3},{3,2},{4,5},{5,4},{6,7},{7,6},{8,10},{9,11},{10,... | collective-permute-start | bytes 1572872 | tf_op jit(solution)/shard_map/ppermute | solution.py:24
  3.6 1.4 %shard_map.76 = (f32[32,8,128]{2,1,0:T(8,128)}, f32[10,128]{1,0:T(8,128)}) custom-call(f32[1,8,128]{2,1,0:T(8,128)} %bitcast.9, s32[1,8]{1,0:T(1,128)} %bitcast.10, s32[1,8]{1,0:T(1,128)} %bitcast.11, f32[1,128]{1,0:T(1,128)} %energies.1), custom_call_target="tpu_custom_call" | custom-call | tf_op jit(solution)/shard_map/pallas_call | solution.py:206
  5.0 0.0 copy-start.1
  5.0 4.9 %all-to-all-start = ((f32[32,8,128]{2,1,0:T(8,128)}), f32[32,8,128]{2,1,0:T(8,128)S(1)}, u32[]{:S(2)}, u32[]{:S(2)}) async-start(f32[32,8,128]{2,1,0:T(8,128)} %get-tuple-element.12), calls=%async_computation | async-start | bytes 262144 | tf_op jit(solution)/shard_map/all_to_all | solution.py:226
  10.0 0.0 copy-done.1
  10.0 1.8 %collective-permute-start.1 = (f32[10,128]{1,0:T(8,128)S(1)}, f32[10,128]{1,0:T(8,128)S(1)}, u32[]{:S(2)}, u32[]{:S(2)}) collective-permute-start(f32[10,128]{1,0:T(8,128)S(1)} %copy-done.1), channel_id=1, source_target_pairs={{0,1},{1,0},{2,3},{3,2},{4,5},{5,4},{6,7},{7,6},{8,10},{9,11},{10,... | collective-permute-start | bytes 15368 | tf_op jit(solution)/shard_map/ppermute | solution.py:24
  11.8 0.0 copy-start
  11.8 1.0 %copy-done = f32[8,1,128,128]{3,2,1,0:T(8,128)S(1)} copy-done((f32[8,1,128,128]{3,2,1,0:T(8,128)S(1)}, f32[8,1,128,128]{3,2,1,0:T(8,128)}, u32[]{:S(2)}) %copy-start) | copy-done | bytes 524312
  12.9 0.2 shard_map.77.halves
  13.0 0.7 %collective-permute-done.1.side.other_side = f32[10,128]{1,0:T(8,128)S(1)} collective-permute-done((f32[10,128]{1,0:T(8,128)S(1)}, f32[10,128]{1,0:T(8,128)S(1)}, u32[]{:S(2)}, u32[]{:S(2)}) %collective-permute-start.1) | collective-permute-done | bytes 5152 | tf_op jit(solution)/shard_map/ppermute | solution.py:24
  13.7 0.0 collective-permute-done.couplings
  13.7 0.2 shard_map.78.other_halves
  13.9 3.8 %all-to-all-done.table = f32[32,8,128]{2,1,0:T(8,128)S(1)} async-done(((f32[32,8,128]{2,1,0:T(8,128)}), f32[32,8,128]{2,1,0:T(8,128)S(1)}, u32[]{:S(2)}, u32[]{:S(2)}) %all-to-all-start) | async-done | bytes 131104 | tf_op jit(solution)/shard_map/all_to_all | solution.py:226
  17.7 0.4 %shard_map.79.mine = f32[8,8,128]{2,1,0:T(8,128)S(1)} custom-call(f32[32,8,128]{2,1,0:T(8,128)S(1)} %all-to-all-done.table, bf16[8,1,256,128]{3,2,1,0:T(8,128)(2,1)S(1)} %shard_map.77.halves, f32[10,128]{1,0:T(8,128)S(1)} %copy-done.1, bf16[8,1,256,128]{3,2,1,0:T(8,128)(2,1)S(1)} %shard_map.78.other_halves, f32[10,128]{1,0:T(8,128)S(1)} %collective-permute-done.1.side.other_side), custom_call_target="tpu_custom_call" | custom-call | flops 4194304 | bytes 1048576 | tf_op jit(solution)/shard_map/pallas_call | solution.py:227
  18.1 1.1 %collective-permute-start.2 = (f32[8,8,128]{2,1,0:T(8,128)S(1)}, f32[8,8,128]{2,1,0:T(8,128)S(1)}, u32[]{:S(2)}, u32[]{:S(2)}) collective-permute-start(f32[8,8,128]{2,1,0:T(8,128)S(1)} %shard_map.79.mine), channel_id=1, source_target_pairs={{0,2},{1,3},{2,0},{3,1},{4,6},{5,7},{6,4},{7,5},{8,9},{9,8},{10,11... | collective-permute-start | bytes 98312 | tf_op jit(solution)/shard_map/ppermute | solution.py:24
  19.2 1.0 %collective-permute-start.3 = (f32[8,8,128]{2,1,0:T(8,128)S(1)}, f32[8,8,128]{2,1,0:T(8,128)S(1)}, u32[]{:S(2)}, u32[]{:S(2)}) collective-permute-start(f32[8,8,128]{2,1,0:T(8,128)S(1)} %shard_map.79.mine), channel_id=1, source_target_pairs={{0,4},{1,5},{2,6},{3,7},{4,0},{5,1},{6,2},{7,3},{8,12},{9,13},{10,... | collective-permute-start | bytes 98312 | tf_op jit(solution)/shard_map/ppermute | solution.py:24
  20.2 2.4 %collective-permute-start.4 = (f32[8,8,128]{2,1,0:T(8,128)S(1)}, f32[8,8,128]{2,1,0:T(8,128)S(1)}, u32[]{:S(2)}, u32[]{:S(2)}) collective-permute-start(f32[8,8,128]{2,1,0:T(8,128)S(1)} %shard_map.79.mine), channel_id=1, source_target_pairs={{0,6},{1,7},{2,4},{3,5},{4,2},{5,3},{6,0},{7,1},{8,13},{9,12},{10,... | collective-permute-start | bytes 98312 | tf_op jit(solution)/shard_map/ppermute | solution.py:24
  22.6 0.9 %shard_map.80.refs_4_ = f32[24,128]{1,0:T(8,128)S(1)} custom-call(f32[32,8,128]{2,1,0:T(8,128)S(1)} %all-to-all-done.table), custom_call_target="tpu_custom_call" | custom-call | flops 1000000 | bytes 131072 | tf_op jit(solution)/shard_map/pallas_call | solution.py:230
  23.5 0.0 collective-permute-done.2.near
  23.5 1.4 %collective-permute-done.3.far = f32[8,8,128]{2,1,0:T(8,128)S(1)} collective-permute-done((f32[8,8,128]{2,1,0:T(8,128)S(1)}, f32[8,8,128]{2,1,0:T(8,128)S(1)}, u32[]{:S(2)}, u32[]{:S(2)}) %collective-permute-start.3) | collective-permute-done | bytes 32800 | tf_op jit(solution)/shard_map/ppermute | solution.py:24
  25.0 0.9 %collective-permute-done.4.both = f32[8,8,128]{2,1,0:T(8,128)S(1)} collective-permute-done((f32[8,8,128]{2,1,0:T(8,128)S(1)}, f32[8,8,128]{2,1,0:T(8,128)S(1)}, u32[]{:S(2)}, u32[]{:S(2)}) %collective-permute-start.4) | collective-permute-done | bytes 32800 | tf_op jit(solution)/shard_map/ppermute | solution.py:24
  25.9 0.2 shard_map.81
  26.1 0.0 collective-permute-start.5
  26.1 1.3 %collective-permute-start.6 = (f32[8,128]{1,0:T(8,128)S(1)}, f32[8,128]{1,0:T(8,128)S(1)}, u32[]{:S(2)}, u32[]{:S(2)}) collective-permute-start(f32[8,128]{1,0:T(8,128)S(1)} %get-tuple-element.15.refs_3_), channel_id=1, source_target_pairs={{0,16},{8,24},{16,0},{24,8},{1,17},{9,25},{17,1},{25,9},{2,18},{10... | collective-permute-start | bytes 12296 | tf_op jit(solution)/shard_map/ppermute | solution.py:14
  27.4 0.6 %collective-permute-start.7 = (f32[8,128]{1,0:T(8,128)S(1)}, f32[8,128]{1,0:T(8,128)S(1)}, u32[]{:S(2)}, u32[]{:S(2)}) collective-permute-start(f32[8,128]{1,0:T(8,128)S(1)} %get-tuple-element.15.refs_3_), channel_id=1, source_target_pairs={{0,8},{8,0},{16,24},{24,16},{1,9},{9,1},{17,25},{25,17},{2,10},{10... | collective-permute-start | bytes 12296 | tf_op jit(solution)/shard_map/ppermute | solution.py:14
  28.0 1.2 %collective-permute-done.5.refs_0_ = f32[8,128]{1,0:T(8,128)S(1)} collective-permute-done((f32[8,128]{1,0:T(8,128)S(1)}, f32[8,128]{1,0:T(8,128)S(1)}, u32[]{:S(2)}, u32[]{:S(2)}) %collective-permute-start.5) | collective-permute-done | bytes 4128 | tf_op jit(solution)/shard_map/ppermute | solution.py:14
  29.1 0.6 %collective-permute-done.6.refs_1_ = f32[8,128]{1,0:T(8,128)S(1)} collective-permute-done((f32[8,128]{1,0:T(8,128)S(1)}, f32[8,128]{1,0:T(8,128)S(1)}, u32[]{:S(2)}, u32[]{:S(2)}) %collective-permute-start.6) | collective-permute-done | bytes 4128 | tf_op jit(solution)/shard_map/ppermute | solution.py:14
  29.8 0.0 collective-permute-done.7.refs_2_
  29.8 0.7 %shard_map.82 = (f32[1,8,128]{2,1,0:T(8,128)}, f32[1,8,128]{2,1,0:T(8,128)}, f32[8]{0:T(128)}) custom-call(f32[8,128]{1,0:T(8,128)S(1)} %collective-permute-done.5.refs_0_, f32[8,128]{1,0:T(8,128)S(1)} %collective-permute-done.6.refs_1_, f32[8,128]{1,0:T(8,128)S(1)} %collective-permute-done.7.refs_2_, f32[8,128]{1,0:T(8,128)S(1)} %get-tuple-element.15.refs_3_, ...), custom_call_target="tpu_custom_call" | custom-call | flops 10000 | bytes 100000 | tf_op jit(solution)/shard_map/pallas_call | solution.py:253
Async XLA Ops:
  0.6 13.1 %collective-permute-start = (f32[8,1,128,128]{3,2,1,0:T(8,128)}, f32[8,1,128,128]{3,2,1,0:T(8,128)S(1)}, u32[]{:S(2)}, u32[]{:S(2)}) collective-permute-start(f32[8,1,128,128]{3,2,1,0:T(8,128)} %couplings.1), channel_id=1, source_target_pairs={{0,1},{1,0},{2,3},{3,2},{4,5},{5,4},{6,7},{7,6},{8,10},{9,11},{10,... | collective-permute-start | bytes 1572872 | tf_op jit(solution)/shard_map/ppermute | solution.py:24
  5.0 4.9 %copy-start.1 = (f32[10,128]{1,0:T(8,128)S(1)}, f32[10,128]{1,0:T(8,128)}, u32[]{:S(2)}) copy-start(f32[10,128]{1,0:T(8,128)} %get-tuple-element.13.side) | copy-start | bytes 15364
  5.0 12.7 %all-to-all-start = ((f32[32,8,128]{2,1,0:T(8,128)}), f32[32,8,128]{2,1,0:T(8,128)S(1)}, u32[]{:S(2)}, u32[]{:S(2)}) async-start(f32[32,8,128]{2,1,0:T(8,128)} %get-tuple-element.12), calls=%async_computation | async-start | bytes 262144 | tf_op jit(solution)/shard_map/all_to_all | solution.py:226
  10.0 3.7 %collective-permute-start.1 = (f32[10,128]{1,0:T(8,128)S(1)}, f32[10,128]{1,0:T(8,128)S(1)}, u32[]{:S(2)}, u32[]{:S(2)}) collective-permute-start(f32[10,128]{1,0:T(8,128)S(1)} %copy-done.1), channel_id=1, source_target_pairs={{0,1},{1,0},{2,3},{3,2},{4,5},{5,4},{6,7},{7,6},{8,10},{9,11},{10,... | collective-permute-start | bytes 15368 | tf_op jit(solution)/shard_map/ppermute | solution.py:24
  11.8 1.0 %copy-start = (f32[8,1,128,128]{3,2,1,0:T(8,128)S(1)}, f32[8,1,128,128]{3,2,1,0:T(8,128)}, u32[]{:S(2)}) copy-start(f32[8,1,128,128]{3,2,1,0:T(8,128)} %couplings.1) | copy-start | bytes 1572868
  18.1 5.4 %collective-permute-start.2 = (f32[8,8,128]{2,1,0:T(8,128)S(1)}, f32[8,8,128]{2,1,0:T(8,128)S(1)}, u32[]{:S(2)}, u32[]{:S(2)}) collective-permute-start(f32[8,8,128]{2,1,0:T(8,128)S(1)} %shard_map.79.mine), channel_id=1, source_target_pairs={{0,2},{1,3},{2,0},{3,1},{4,6},{5,7},{6,4},{7,5},{8,9},{9,8},{10,11... | collective-permute-start | bytes 98312 | tf_op jit(solution)/shard_map/ppermute | solution.py:24
  19.2 5.8 %collective-permute-start.3 = (f32[8,8,128]{2,1,0:T(8,128)S(1)}, f32[8,8,128]{2,1,0:T(8,128)S(1)}, u32[]{:S(2)}, u32[]{:S(2)}) collective-permute-start(f32[8,8,128]{2,1,0:T(8,128)S(1)} %shard_map.79.mine), channel_id=1, source_target_pairs={{0,4},{1,5},{2,6},{3,7},{4,0},{5,1},{6,2},{7,3},{8,12},{9,13},{10,... | collective-permute-start | bytes 98312 | tf_op jit(solution)/shard_map/ppermute | solution.py:24
  20.2 5.7 %collective-permute-start.4 = (f32[8,8,128]{2,1,0:T(8,128)S(1)}, f32[8,8,128]{2,1,0:T(8,128)S(1)}, u32[]{:S(2)}, u32[]{:S(2)}) collective-permute-start(f32[8,8,128]{2,1,0:T(8,128)S(1)} %shard_map.79.mine), channel_id=1, source_target_pairs={{0,6},{1,7},{2,4},{3,5},{4,2},{5,3},{6,0},{7,1},{8,13},{9,12},{10,... | collective-permute-start | bytes 98312 | tf_op jit(solution)/shard_map/ppermute | solution.py:24
  26.1 3.0 %collective-permute-start.5 = (f32[8,128]{1,0:T(8,128)S(1)}, f32[8,128]{1,0:T(8,128)S(1)}, u32[]{:S(2)}, u32[]{:S(2)}) collective-permute-start(f32[8,128]{1,0:T(8,128)S(1)} %get-tuple-element.15.refs_3_), channel_id=1, source_target_pairs={{0,24},{8,16},{16,8},{24,0},{1,25},{9,17},{17,9},{25,1},{2,26},{10... | collective-permute-start | bytes 12296 | tf_op jit(solution)/shard_map/ppermute | solution.py:14
  26.1 3.7 %collective-permute-start.6 = (f32[8,128]{1,0:T(8,128)S(1)}, f32[8,128]{1,0:T(8,128)S(1)}, u32[]{:S(2)}, u32[]{:S(2)}) collective-permute-start(f32[8,128]{1,0:T(8,128)S(1)} %get-tuple-element.15.refs_3_), channel_id=1, source_target_pairs={{0,16},{8,24},{16,0},{24,8},{1,17},{9,25},{17,1},{25,9},{2,18},{10... | collective-permute-start | bytes 12296 | tf_op jit(solution)/shard_map/ppermute | solution.py:14
  27.4 2.4 %collective-permute-start.7 = (f32[8,128]{1,0:T(8,128)S(1)}, f32[8,128]{1,0:T(8,128)S(1)}, u32[]{:S(2)}, u32[]{:S(2)}) collective-permute-start(f32[8,128]{1,0:T(8,128)S(1)} %get-tuple-element.15.refs_3_), channel_id=1, source_target_pairs={{0,8},{8,0},{16,24},{24,16},{1,9},{9,1},{17,25},{25,17},{2,10},{10... | collective-permute-start | bytes 12296 | tf_op jit(solution)/shard_map/ppermute | solution.py:14
